TPU v7x, 32 devices: a whole 2x2x4 slice. The times are simulated.
32 devices in a mesh: gx: 8 (over z, x), gy: 4 (over y, core).
Axes of the slice: x: 2, y: 2, z: 4, core: 2. Of those that a mesh axis runs over, the one named last changes fastest.
Arguments:
- factor_grads: bfloat16 [128, 196608], P(('gx', 'gy')), may hold values from -0.29882812 to 0.29882812
- latents: bfloat16 [128, 1024], P(('gx', 'gy')), may hold values from -6 to 6
- task_ids: int32 [128], P(('gx', 'gy')), may hold values from 0 to 127, each once
- offsets: int32 [160], replicated, may hold values from 0 to 196607, as said below
- target_scale: float32 [160], replicated, may hold values from 0.5 to 2
- momentum: float32 [1024, 196608], P(None, ('gx', 'gy')), may hold values from -6 to 6
Outputs:
- new_momentum: float32 [1024, 196608], P(None, ('gx', 'gy'))
- step: float32 [1024, 196608], P(None, ('gx', 'gy'))
Inputs may be any that keep to these rules, and one draw needn't show every extreme that they name: `task_ids`: a permutation of 0 to 127. offsets[0] is 0 and offsets rise strictly.
All inputs are finite; a program needn't handle non-finite values.
Results may differ from a plain program's by a relative error of at most 0.0003.
Values may be sent and summed in bfloat16 or wider, within the bound.
No kernel may reach another device: no remote copies, remote signals or barrier semaphores. Data moves between devices by JAX's collectives and lax.ppermute only.
A program may use at most 192 MiB of HBM per device.

v0:
```python
import math

import jax
import jax.numpy as jnp
from jax import lax
from jax.sharding import PartitionSpec as P

OUT = 196608
ITERS = 2


MOMENTUM_DECAY = 0.95
EPSILON = 1e-07
NEWTON_A = 3.4445
NEWTON_B = -4.775
NEWTON_C = 2.0315


def local_gram(matrix):
    return lax.dot_general(
        matrix,
        matrix,
        (((1,), (1,)), ((), ())),
        precision=lax.Precision.HIGHEST,
        preferred_element_type=jnp.float32,
    )


def summed_gram(matrix):
    partial_gram = local_gram(matrix)
    return lax.psum(partial_gram, ("gx", "gy"))


def per_device(factor_grads, latents, task_ids, offsets, target_scale, momentum):
    all_latents, all_ids = (
        lax.all_gather(latents, ("gx", "gy"), axis=0, tiled=True),
        lax.all_gather(task_ids, ("gx", "gy"), axis=0, tiled=True),
    )
    columns = lax.all_to_all(factor_grads, ("gx", "gy"), split_axis=1, concat_axis=0, tiled=True)
    task_latent = all_latents[all_ids]
    head_grad = lax.dot_general(
        task_latent, columns, (((0,), (0,)), ((), ())), preferred_element_type=jnp.float32
    )
    new_momentum = MOMENTUM_DECAY * momentum + head_grad
    blended = head_grad + MOMENTUM_DECAY * new_momentum
    squares = lax.psum(jnp.sum(blended * blended), ("gx", "gy"))
    frobenius = jnp.sqrt(squares)
    orthogonal = blended / (frobenius + EPSILON)
    device_count = lax.axis_size(("gx", "gy"))
    block_rows = orthogonal.shape[0] // device_count
    first_row = lax.axis_index(("gx", "gy")) * block_rows
    for iteration in range(ITERS):
        gram_matrix = summed_gram(orthogonal)
        gram_rows = lax.dynamic_slice_in_dim(gram_matrix, first_row, block_rows, 0)
        poly_rows = NEWTON_B * gram_rows + NEWTON_C * jnp.dot(
            gram_rows, gram_matrix, precision=lax.Precision.HIGHEST
        )
        current = orthogonal
        portion = lax.all_gather(
            poly_rows.astype(jnp.bfloat16), ("gx", "gy"), axis=0, tiled=True
        ).astype(jnp.float32)
        leading = lax.slice_in_dim(current, 0, portion.shape[0], axis=0)
        orthogonal = NEWTON_A * leading + jnp.dot(portion, current, precision=lax.Precision.HIGHEST)
    column_count = orthogonal.shape[1]
    column_index = lax.axis_index(("gx", "gy")) * column_count + jnp.arange(
        column_count, dtype=jnp.int32
    )
    beyond = (column_index[:, None] >= offsets[None, :]).astype(jnp.float32)
    deltas = target_scale - jnp.concatenate([jnp.zeros((1,), jnp.float32), target_scale[:-1]])
    column_scale = jnp.sum(beyond * deltas[None, :], axis=1)
    step = math.sqrt(OUT) * column_scale[None, :] * orthogonal
    return (new_momentum, step)


def solution(mesh):
    placed = (
        P(("gx", "gy"), None),
        P(("gx", "gy"), None),
        P(("gx", "gy")),
        P(),
        P(),
        P(None, ("gx", "gy")),
    )
    return jax.shard_map(
        per_device,
        mesh=mesh,
        in_specs=placed,
        out_specs=(P(None, ("gx", "gy")), P(None, ("gx", "gy"))),
        check_vma=False,
    )
```

profile of v0, /device:TPU:0, one launch (start us, length us, event | category | flops | bytes accessed | tf_op | source)
XLA Modules:
  0.0 876.6 jit_solution(16040109965922447686)
XLA Ops:
  7.2 7.3 all-to-all-start
  14.5 0.0 all-reduce.4.cloned.1.call-start
  14.5 61.6 %all-gather = bf16[32,4,1024]{2,1,0:T(4,128)(2,1)S(1)} all-gather(bf16[1,4,1024]{2,1,0:T(4,128)(2,1)} %bitcast.16), channel_id=1, replica_groups=mesh['gx'=8,'gy'=4] {'gx','gy'}, dimensions={0}, use_global_device_ids=true | all-gather | bytes 270336 | tf_op jit(solution)/shard_map/all_gather | solution.py:36
  76.2 0.1 reshape.29
  76.2 0.9 dynamic-update-slice
  77.1 40.4 %all-reduce = s32[128]{0:T(128)S(1)} all-reduce(s32[128]{0:T(128)S(1)} %dynamic-update-slice), channel_id=1, replica_groups=mesh['gx'=8,'gy'=4] {'gx','gy'}, use_global_device_ids=true, to_apply=%add | all-reduce | flops 128 | bytes 1024
  117.5 0.9 gather_fusion
  118.4 0.0 all-to-all-done
  118.4 0.4 all_to_all.17
  118.8 24.5 %multiply_reduce_fusion = (f32[]{:T(128)}, f32[1024,6144]{1,0:T(8,128)}, f32[1024,6144]{1,0:T(8,128)}) fusion(f32[1024,6144]{1,0:T(8,128)} %param.11, bf16[128,1024]{1,0:T(8,128)(2,1)S(1)} %gather_fusion, bf16[128,6144]{1,0:T(8,128)(2,1)S(1)} %all_to_all.17), kind=kOutput, calls=%fused_computation.3 | convolution fusion | flops 1648361472 | bytes 77332480 | tf_op jit(solution)/shard_map/dot_general | solution.py:41
  143.4 39.7 %psum.21 = f32[]{:T(128)} all-reduce(f32[]{:T(128)} %get-tuple-element.2), channel_id=1, replica_groups=mesh['gx'=8,'gy'=4] {'gx','gy'}, use_global_device_ids=true, to_apply=%region_2.0 | all-reduce | flops 1 | bytes 8 | tf_op jit(solution)/shard_map/psum | solution.py:46
  183.6 92.8 %fusion = f32[1024,1024]{1,0:T(8,128)} fusion(f32[]{:T(128)S(6)} %add.58, f32[1024,6144]{1,0:T(8,128)} %get-tuple-element.4, f32[1024,6144]{1,0:T(8,128)} %get-tuple-element.3), kind=kOutput, calls=%fused_computation.7 | convolution fusion | flops 77328285696 | bytes 54525956 | tf_op jit(solution)/shard_map/dot_general | solution.py:20
  276.4 0.0 all-reduce.4.cloned.1.call-update
  276.4 0.2 all-gather.4.cloned.1.call-start
  276.6 142.7 %all-reduce.4.cloned.1.call-done = f32[1024,1024]{1,0:T(8,128)} async-done(((f32[1024,1024]{1,0:T(8,128)}), f32[1024,1024]{1,0:T(8,128)}) %all-reduce.4.cloned.1.call-update) | async-done | bytes 4194320 | tf_op jit(solution)/shard_map/psum | solution.py:31
  419.4 5.3 fusion.3
  424.7 0.0 all-gather.4.cloned.1.call-update
  424.7 0.0 all-reduce.6.cloned.1.call-start
  424.8 55.4 %all-gather.4.cloned.1.call-done = bf16[1024,1024]{1,0:T(8,128)(2,1)} async-done(((bf16[32,1024]{1,0:T(8,128)(2,1)}), bf16[1024,1024]{1,0:T(8,128)(2,1)}) %all-gather.4.cloned.1.call-update) | async-done | bytes 2097168 | tf_op jit(solution)/shard_map/all_gather | solution.py:59
  480.2 52.7 %multiply_add_fusion = f32[1024,6144]{1,0:T(8,128)} fusion(bf16[1024,1024]{1,0:T(8,128)(2,1)} %all-gather.4.cloned.1.call-done, f32[]{:T(128)S(6)} %add.58, f32[1024,6144]{1,0:T(8,128)} %get-tuple-element.4, f32[1024,6144]{1,0:T(8,128)} %get-tuple-element.3), kind=kOutput, calls=%fused_computation.2 | convolution fusion | flops 77359742976 | bytes 77594624 | tf_op jit(solution)/shard_map/dot_general | solution.py:63
  532.9 0.0 copy-start
  532.9 0.0 copy-start.1
  532.9 87.5 %fusion.9 = f32[1024,1024]{1,0:T(8,128)} fusion(f32[1024,6144]{1,0:T(8,128)} %multiply_add_fusion), kind=kOutput, calls=%fused_computation.24 | convolution fusion | flops 77309411328 | bytes 29360128 | tf_op jit(solution)/shard_map/dot_general | solution.py:20
  620.3 0.0 all-reduce.6.cloned.1.call-update
  620.4 0.0 all-gather.6.cloned.1.call-start
  620.4 140.7 %all-reduce.6.cloned.1.call-done = f32[1024,1024]{1,0:T(8,128)} async-done(((f32[1024,1024]{1,0:T(8,128)}), f32[1024,1024]{1,0:T(8,128)}) %all-reduce.6.cloned.1.call-update) | async-done | bytes 4194320 | tf_op jit(solution)/shard_map/psum | solution.py:31
  761.1 5.3 fusion.4
  766.4 0.0 all-gather.6.cloned.1.call-update
  766.5 0.0 copy-done
  766.5 0.1 maximum_subtract_fusion
  766.6 0.0 copy-done.1
  766.6 0.5 select_reduce_fusion
  767.1 54.8 %all-gather.6.cloned.1.call-done = bf16[1024,1024]{1,0:T(8,128)(2,1)} async-done(((bf16[32,1024]{1,0:T(8,128)(2,1)}), bf16[1024,1024]{1,0:T(8,128)(2,1)}) %all-gather.6.cloned.1.call-update) | async-done | bytes 2097168 | tf_op jit(solution)/shard_map/all_gather | solution.py:59
  821.9 47.9 %add_multiply_fusion = f32[1024,6144]{1,0:T(8,128)} fusion(f32[1024,6144]{1,0:T(8,128)} %multiply_add_fusion, bf16[1024,1024]{1,0:T(8,128)(2,1)} %all-gather.6.cloned.1.call-done, f32[6144]{0:T(1024)S(1)} %broadcast_multiply_fusion), kind=kOutput, calls=%fused_computation.1 | convolution fusion | flops 77328285696 | bytes 52453376 | tf_op jit(solution)/shard_map/dot_general | solution.py:63
  (5 shorter events, 0.0 us)
Async XLA Ops:
  7.2 111.2 %all-to-all-start = ((bf16[4,32,6144]{2,0,1:T(4,128)(2,1)}), bf16[4,32,6144]{2,0,1:T(4,128)(2,1)S(1)}, u32[]{:S(2)}, u32[]{:S(2)}) async-start(bf16[4,32,6144]{2,0,1:T(4,128)(2,1)} %bitcast.15), calls=%async_computation | async-start | bytes 3145728 | tf_op jit(solution)/shard_map/all_to_all | solution.py:39
  14.5 404.9 %all-reduce.4.cloned.1.call-start = ((), (), s32[]{:S(2)}) async-start(), calls=%async_computation.1 | async-start | bytes 8388608 | tf_op jit(solution)/shard_map/psum | solution.py:31
  276.4 203.7 %all-gather.4.cloned.1.call-start = ((), (), s32[]{:S(2)}) async-start(), calls=%async_computation.2 | async-start | bytes 2162688 | tf_op jit(solution)/shard_map/all_gather | solution.py:59
  424.7 336.4 %all-reduce.6.cloned.1.call-start = ((), (), s32[]{:S(2)}) async-start(), calls=%async_computation.3 | async-start | bytes 8388608 | tf_op jit(solution)/shard_map/psum | solution.py:31
  532.9 233.6 %copy-start = (f32[160]{0:T(256)S(1)}, f32[160]{0:T(256)}, u32[]{:S(2)}) copy-start(f32[160]{0:T(256)} %param.10) | copy-start | bytes 1924
  532.9 233.7 %copy-start.1 = (s32[160]{0:T(256)S(1)}, s32[160]{0:T(256)}, u32[]{:S(2)}) copy-start(s32[160]{0:T(256)} %param.9) | copy-start | bytes 1924
  620.4 201.5 %all-gather.6.cloned.1.call-start = ((), (), s32[]{:S(2)}) async-start(), calls=%async_computation.4 | async-start | bytes 2162688 | tf_op jit(solution)/shard_map/all_gather | solution.py:59
Sparse Core Ops, SparseCore 0:
  276.5 142.7 all-reduce.3
  424.8 55.2 all-gather.3
  620.5 140.5 all-reduce.5
  766.6 55.2 all-gather.5
where the time goes:
time: 881 us; the launch traced here: 877 us
  waiting for transfers between devices  394 us (45%)
  matrix products  316 us (36%)
  blocking collectives  142 us (16%)
  between operations  14.7 us (2%)
    psum x2, waiting for transfers between devices, summed_gram(): return lax.psum(partial_gram, ('gx', 'gy'))  283 us
    dot_general x2, matrix products, local_gram(): lax.dot_general(matrix, matrix, (((1,), (1,)), ((), ())), precision=lax.P...  180 us
    all_gather x2, waiting for transfers between devices, per_device(): lax.all_gather(poly_rows.astype(jnp.bfloat16), ('gx', 'gy'), axis=0, tile...  110 us
    dot_general x2, matrix products, per_device(): jnp.dot(portion, current, precision=lax.Precision.HIGHEST)  101 us
    all_gather x1, blocking collectives, per_device(): lax.all_gather(latents, ('gx', 'gy'), axis=0, tiled=True)  61.6 us
    unnamed x1, blocking collectives  40.4 us
    psum x1, blocking collectives, per_device(): squares = lax.psum(jnp.sum(blended * blended), ('gx', 'gy'))  39.7 us
    dot_general x1, matrix products, per_device(): lax.dot_general(task_latent, columns, (((0,), (0,)), ((), ())), preferred...  24.5 us
  transfers between devices with their start and end apart: 5, of which 4 were waited for; matrix products, arithmetic and copies ran while one was open for 0% of the time, Pallas kernels for 0%

commit v1 on v0

v1 whole, which is shorter than its diff:
```python
import functools
import math

import jax
import jax.numpy as jnp
from jax import lax
from jax.experimental import pallas as pl
from jax.experimental.pallas import tpu as pltpu
from jax.sharding import PartitionSpec as P

MOMENTUM_DECAY = 0.95
EPSILON = 1e-07
NEWTON_A = 3.4445
NEWTON_B = -4.775
NEWTON_C = 2.0315

AXES = ("gx", "gy")
BLOCK = 256
LANES = 128
PIECES = 3
PIECES_AT = (1, 2)
SMALL = pl.CostEstimate(flops=1, bytes_accessed=1, transcendentals=0)
F32 = jnp.float32
BF16 = jnp.bfloat16


def dot(a, b):
    return jnp.dot(a, b, preferred_element_type=F32)


def dot_nt(a, b):
    return lax.dot_general(a, b, (((1,), (1,)), ((), ())), preferred_element_type=F32)


def swap(x, distance, count):
    return lax.ppermute(x, AXES, [(i, i ^ distance) for i in range(count)])


def upper_blocks(size):
    return [(i, j) for i in range(size) for j in range(i, size)]


def column_tile(columns, limit):
    return max(t for t in range(LANES, limit + 1, LANES) if columns % t == 0)


def with_ids(latents, task_ids):
    id_columns = jnp.stack([task_ids // 256, task_ids % 256], axis=1).astype(BF16)
    return jnp.concatenate([latents, jnp.pad(id_columns, ((0, 0), (0, LANES - 2)))], axis=1)


def chosen_latents(held, me, rows, width):
    tasks = held.shape[0]
    place = jnp.arange(tasks, dtype=jnp.int32)
    origin = ((place // rows) ^ me) * rows + place % rows
    held_ids = held[:, width].astype(jnp.int32) * 256 + held[:, width + 1].astype(jnp.int32)
    ids = jnp.sum(jnp.where(origin[None, :] == place[:, None], held_ids[None, :], 0), axis=1)
    chosen = (ids[:, None] == origin[None, :]).astype(BF16)
    return dot(chosen, held[:, :width]).astype(BF16)


def tie_kernel(x_ref, after_ref, out_ref):
    del x_ref, after_ref, out_ref


def tied(x, after):
    anywhere = pl.BlockSpec(memory_space=pl.ANY)
    return pl.pallas_call(
        tie_kernel,
        in_specs=[anywhere, anywhere],
        out_specs=anywhere,
        out_shape=jax.ShapeDtypeStruct(x.shape, x.dtype),
        input_output_aliases={0: 0},
        cost_estimate=SMALL,
        name="tie",
    )(x, after)


def summed(x):
    return jnp.sum(jnp.sum(x, axis=1, keepdims=True), axis=0, keepdims=True)


def gram_kernel(momentum_ref, rounded_ref, gram_ref, note_ref, squares_ref):
    step = pl.program_id(0)

    @pl.when(step == 0)
    def _():
        gram_ref[...] = jnp.zeros_like(gram_ref)
        squares_ref[...] = jnp.zeros_like(squares_ref)

    momentum = momentum_ref[...]
    size, tile = momentum.shape
    squares_ref[...] += jnp.sum((momentum * momentum).reshape(size // 8, 8, tile), axis=0)
    rounded = momentum.astype(BF16)
    rounded_ref[...] = rounded
    for at, (i, j) in enumerate(upper_blocks(size // BLOCK)):
        gram_ref[at * BLOCK : (at + 1) * BLOCK, :] += dot_nt(
            rounded[i * BLOCK : (i + 1) * BLOCK], rounded[j * BLOCK : (j + 1) * BLOCK]
        )

    @pl.when(step == pl.num_programs(0) - 1)
    def _():
        note_ref[...] = jnp.broadcast_to(summed(squares_ref[...]), note_ref.shape)


def gram_pass(momentum):
    size, count = momentum.shape
    tile = column_tile(count, 1024)
    packed = len(upper_blocks(size // BLOCK)) * BLOCK
    return pl.pallas_call(
        gram_kernel,
        grid=(count // tile,),
        in_specs=[pl.BlockSpec((size, tile), lambda i: (0, i))],
        out_specs=[
            pl.BlockSpec((size, tile), lambda i: (0, i)),
            pl.BlockSpec((packed, BLOCK), lambda i: (0, 0)),
            pl.BlockSpec((8, LANES), lambda i: (0, 0)),
        ],
        out_shape=[
            jax.ShapeDtypeStruct((size, count), BF16),
            jax.ShapeDtypeStruct((packed, BLOCK), F32),
            jax.ShapeDtypeStruct((8, LANES), F32),
        ],
        scratch_shapes=[pltpu.VMEM((8, tile), F32)],
        compiler_params=pltpu.CompilerParams(vmem_limit_bytes=56 * 2**20),
        cost_estimate=SMALL,
        name="momentum_gram",
    )(momentum)


def cross_kernel(columns_ref, rounded_ref, cross_ref):
    size = rounded_ref.shape[0]

    @pl.when(pl.program_id(0) == 0)
    def _():
        cross_ref[...] = jnp.zeros_like(cross_ref)

    columns = columns_ref[...]
    cross_ref[:, :size] += dot_nt(columns, rounded_ref[...])
    cross_ref[:, size:] += dot_nt(columns, columns)


def cross_pass(columns, rounded):
    size, count = rounded.shape
    tasks = columns.shape[0]
    tile = column_tile(count, 2048)
    return pl.pallas_call(
        cross_kernel,
        grid=(count // tile,),
        in_specs=[
            pl.BlockSpec((tasks, tile), lambda i: (0, i)),
            pl.BlockSpec((size, tile), lambda i: (0, i)),
        ],
        out_specs=pl.BlockSpec((tasks, size + tasks), lambda i: (0, 0)),
        out_shape=jax.ShapeDtypeStruct((tasks, size + tasks), F32),
        compiler_params=pltpu.CompilerParams(vmem_limit_bytes=60 * 2**20),
        cost_estimate=pl.CostEstimate(
            flops=2 * size * tasks * count, bytes_accessed=2 * size * count, transcendentals=0
        ),
        name="cross_terms",
    )(columns, rounded)


def parted(x):
    high = x.astype(BF16)
    return high, (x - high.astype(F32)).astype(BF16)


def blended_kernel(side_ref, cross_ref, latent_ref, momentum_gram_ref, squares_ref, kept_ref, sent_ref, note_ref, gram_ref):
    tasks, size = latent_ref.shape
    alpha, beta = MOMENTUM_DECAY**2, 1.0 + MOMENTUM_DECAY
    latent = latent_ref[...]
    turned = latent.astype(F32).T.astype(BF16)
    twice = jnp.concatenate([latent, latent], axis=0)
    shares = jnp.concatenate(parted(cross_ref[:, size:]), axis=1)
    mixed = alpha * beta * cross_ref[:, :size] + 0.5 * beta * beta * dot(shares, twice)
    right = jnp.concatenate([twice, *parted(mixed)], axis=0)
    left = jnp.concatenate([*parted(mixed.T), turned, turned], axis=1)
    for at, (i, j) in enumerate(upper_blocks(size // BLOCK)):
        block = slice(at * BLOCK, (at + 1) * BLOCK)
        gram_ref[block, :] = alpha * alpha * momentum_gram_ref[block, :] + dot(
            left[i * BLOCK : (i + 1) * BLOCK, :], right[:, j * BLOCK : (j + 1) * BLOCK]
        )
    half = kept_ref.shape[0]
    side = side_ref[0]
    kept_ref[...] = gram_ref[pl.ds(pl.multiple_of(side * half, half), half), :]
    sent_ref[...] = gram_ref[pl.ds(pl.multiple_of((1 - side) * half, half), half), :].astype(BF16)

    total = alpha * alpha * squares_ref[0:1, 0:1] + 2.0 * summed(mixed * latent.astype(F32))
    total = jnp.broadcast_to(total, note_ref.shape)
    high = total.astype(BF16).astype(F32)
    middle = (total - high).astype(BF16).astype(F32)
    lane = lax.broadcasted_iota(jnp.int32, note_ref.shape, 1)
    note = jnp.where(
        lane == 0, high, jnp.where(lane == 1, middle, jnp.where(lane == 2, total - high - middle, 0.0))
    )
    note_ref[...] = note.astype(BF16)


def blended_gram(side, cross, latent, gram, squares):
    half = gram.shape[0] // 2
    whole = pl.BlockSpec(memory_space=pltpu.VMEM)
    return pl.pallas_call(
        blended_kernel,
        in_specs=[pl.BlockSpec(memory_space=pltpu.SMEM), whole, whole, whole, whole],
        out_specs=[whole, whole, whole],
        out_shape=[
            jax.ShapeDtypeStruct((half, BLOCK), F32),
            jax.ShapeDtypeStruct((half, BLOCK), BF16),
            jax.ShapeDtypeStruct((16, BLOCK), BF16),
        ],
        scratch_shapes=[pltpu.VMEM(gram.shape, F32)],
        compiler_params=pltpu.CompilerParams(vmem_limit_bytes=40 * 2**20),
        cost_estimate=pl.CostEstimate(
            flops=4 * latent.shape[0] * latent.shape[1] ** 2, bytes_accessed=8 * gram.size, transcendentals=0
        ),
        name="blended_gram",
    )(side, cross, latent, gram, squares)


def momentum_kernel(latent_ref, momentum_ref, columns_ref, *refs):
    new_ref, mark_ref = refs[-2:]
    head_grad = lax.dot_general(
        latent_ref[...], columns_ref[...], (((0,), (0,)), ((), ())), preferred_element_type=F32
    )
    new_ref[...] = MOMENTUM_DECAY * momentum_ref[...] + head_grad
    mark_ref[...] = jnp.zeros_like(mark_ref)


def momentum_piece(latent, momentum, columns, after, held, piece, pieces):
    size, count = momentum.shape
    tasks = columns.shape[0]
    tile = column_tile(count // pieces, 1024)
    steps = count // pieces // tile
    first = piece * steps
    anywhere = pl.BlockSpec(memory_space=pl.ANY)
    operands = (latent, momentum, columns, after) + (() if held is None else (held,))
    return pl.pallas_call(
        momentum_kernel,
        grid=(steps,),
        in_specs=[
            pl.BlockSpec((tasks, size), lambda i: (0, 0)),
            pl.BlockSpec((size, tile), lambda i: (0, i + first)),
            pl.BlockSpec((tasks, tile), lambda i: (0, i + first)),
        ]
        + [anywhere] * (len(operands) - 3),
        out_specs=[
            pl.BlockSpec((size, tile), lambda i: (0, i + first)),
            pl.BlockSpec((8, LANES), lambda i: (0, 0)),
        ],
        out_shape=[
            jax.ShapeDtypeStruct((size, count), F32),
            jax.ShapeDtypeStruct((8, LANES), F32),
        ],
        input_output_aliases={} if held is None else {4: 0},
        compiler_params=pltpu.CompilerParams(vmem_limit_bytes=56 * 2**20),
        cost_estimate=SMALL,
        name="new_momentum",
    )(*operands)


def poly_kernel(notes_ref, gram_ref, latent_ref, weight_ref, inverse_ref, x_ref, xb_ref, p_ref, pb_ref, d_ref):
    size = x_ref.shape[0]
    tasks = latent_ref.shape[0]
    blocks = size // BLOCK
    a, b, c = NEWTON_A, NEWTON_B, NEWTON_C
    beta = 1.0 + MOMENTUM_DECAY

    def part(i):
        return slice(i * BLOCK, (i + 1) * BLOCK)

    turned = latent_ref[...].astype(F32).T.astype(BF16)
    norm = jnp.sqrt(jnp.maximum(summed(notes_ref[...].astype(F32)), 0.0)) + EPSILON
    inverse_ref[...] = jnp.broadcast_to(1.0 / norm, inverse_ref.shape)
    inverse = 1.0 / (norm * norm)

    for at, (i, j) in enumerate(upper_blocks(blocks)):
        block = gram_ref[part(at), :].astype(F32) * inverse
        x_ref[part(i), part(j)] = block
        xb_ref[part(i), part(j)] = block.astype(BF16)
        if i != j:
            x_ref[part(j), part(i)] = block.T
            xb_ref[part(j), part(i)] = block.T.astype(BF16)
    for j in range(blocks):
        poly = b * x_ref[:, part(j)] + c * dot(xb_ref[...], xb_ref[:, part(j)])
        p_ref[:, part(j)] = poly
        pb_ref[:, part(j)] = poly.astype(BF16)
    for j in range(blocks):
        d_ref[:, part(j)] = (
            2 * a * p_ref[:, part(j)] + dot(pb_ref[...], pb_ref[:, part(j)])
        ).astype(BF16)
    for j in range(blocks):
        x_ref[:, part(j)] = a * a * x_ref[:, part(j)] + dot(xb_ref[...], d_ref[:, part(j)])
    xb_ref[...] = x_ref[...].astype(BF16)
    for j in range(blocks):
        poly = b * x_ref[:, part(j)] + c * dot(xb_ref[...], xb_ref[:, part(j)])
        p_ref[:, part(j)] = p_ref[:, part(j)] + poly
        d_ref[:, part(j)] = poly.astype(BF16)
    for j in range(blocks):
        rest = a * p_ref[:, part(j)] + dot(d_ref[...], pb_ref[:, part(j)])
        xb_ref[:, part(j)] = rest.astype(BF16)
        weight_ref[:, part(j)] = (MOMENTUM_DECAY**2 * rest).astype(BF16)
    side = beta * (a * a * turned.astype(F32) + dot(xb_ref[...], turned))
    high = side.astype(BF16)
    weight_ref[:, size : size + tasks] = high
    weight_ref[:, size + tasks :] = (side - high.astype(F32)).astype(BF16)


def poly_pass(notes, gram, latent):
    tasks, size = latent.shape
    whole = pl.BlockSpec(memory_space=pltpu.VMEM)
    return pl.pallas_call(
        poly_kernel,
        in_specs=[whole, whole, whole],
        out_specs=[whole, whole],
        out_shape=[
            jax.ShapeDtypeStruct((size, size + 2 * tasks), BF16),
            jax.ShapeDtypeStruct((8, LANES), F32),
        ],
        scratch_shapes=[
            pltpu.VMEM((size, size), F32),
            pltpu.VMEM((size, size), BF16),
            pltpu.VMEM((size, size), F32),
            pltpu.VMEM((size, size), BF16),
            pltpu.VMEM((size, size), BF16),
        ],
        compiler_params=pltpu.CompilerParams(vmem_limit_bytes=50 * 2**20),
        cost_estimate=pl.CostEstimate(flops=10 * size**3, bytes_accessed=4 * size * size, transcendentals=0),
        name="polynomial",
    )(notes, gram, latent)


def step_kernel(weight_ref, inverse_ref, scale_ref, momentum_ref, columns_ref, step_ref, right_ref):
    momentum = momentum_ref[...]
    size = momentum.shape[0]
    tasks = columns_ref.shape[0]
    right_ref[:size, :] = momentum.astype(BF16)
    right_ref[size : size + tasks, :] = columns_ref[...]
    right_ref[size + tasks :, :] = columns_ref[...]
    factor = NEWTON_A**2 * MOMENTUM_DECAY**2
    scale = scale_ref[...] * inverse_ref[0:1, 0:1]
    step_ref[...] = scale * (factor * momentum + dot(weight_ref[...], right_ref[...]))


def step_pass(weight, inverse, scale, momentum, columns):
    size, count = momentum.shape
    tasks = columns.shape[0]
    depth = weight.shape[1]
    tile = column_tile(count, 1024)
    return pl.pallas_call(
        step_kernel,
        grid=(count // tile,),
        in_specs=[
            pl.BlockSpec((size, depth), lambda i: (0, 0)),
            pl.BlockSpec((8, LANES), lambda i: (0, 0)),
            pl.BlockSpec((1, tile), lambda i: (0, i)),
            pl.BlockSpec((size, tile), lambda i: (0, i)),
            pl.BlockSpec((tasks, tile), lambda i: (0, i)),
        ],
        out_specs=pl.BlockSpec((size, tile), lambda i: (0, i)),
        out_shape=jax.ShapeDtypeStruct((size, count), F32),
        scratch_shapes=[pltpu.VMEM((depth, tile), BF16)],
        compiler_params=pltpu.CompilerParams(vmem_limit_bytes=50 * 2**20),
        cost_estimate=pl.CostEstimate(
            flops=2 * count * size * depth, bytes_accessed=8 * size * count, transcendentals=0
        ),
        name="step",
    )(weight, inverse, scale, momentum, columns)


def halves(gram, distance, me):
    half = gram.shape[0] // 2
    side = (me // distance) % 2
    sent = lax.dynamic_slice_in_dim(gram, (1 - side) * half, half, 0).astype(BF16)
    return lax.dynamic_slice_in_dim(gram, side * half, half, 0), sent


def doubled(gram, got, distance, me):
    side = (me // distance) % 2
    return jnp.concatenate(
        [jnp.where(side == 0, gram, got), jnp.where(side == 0, got, gram)], axis=0
    )


def per_device(out_total, factor_grads, latents, task_ids, offsets, target_scale, momentum):
    count = lax.axis_size(AXES)
    me = lax.axis_index(AXES)
    rows, size = latents.shape
    column_count = momentum.shape[1]
    distances = [2**k for k in range(count.bit_length() - 1)]

    columns = lax.all_to_all(factor_grads, AXES, split_axis=1, concat_axis=0, tiled=True)
    held = with_ids(latents, task_ids)
    rounded, gram, squares = gram_pass(momentum)
    cross = cross_pass(columns, rounded)
    for place, distance in enumerate(distances):
        got = swap(held, distance, count)
        if place == len(distances) - 2:
            got = tied(got, squares)
        if place == len(distances) - 1:
            got = tied(got, cross)
        held = jnp.concatenate([held, got], axis=0)
    latent = chosen_latents(held, me, rows, size)
    side = me % 2
    kept, sent, note = blended_gram(side.astype(jnp.int32).reshape(1), cross, latent, gram, squares)

    new_momentum = None
    for place, distance in enumerate(distances):
        if place > 0:
            kept, sent = halves(gram, distance, me)
        got = swap(sent, distance, count)
        if place in PIECES_AT:
            new_momentum, mark = momentum_piece(
                latent, momentum, columns, sent, new_momentum, place - PIECES_AT[0], PIECES
            )
            got = tied(got, mark)
        gram = kept + got.astype(F32)
    shard = gram.shape[0]
    gram = jnp.concatenate([gram.astype(BF16), note], axis=0)
    for distance in distances[::-1]:
        got = swap(gram, distance, count)
        if distance == 2:
            new_momentum, mark = momentum_piece(
                latent, momentum, columns, gram, new_momentum, PIECES - 1, PIECES
            )
            got = tied(got, mark)
        if distance > 1:
            gram = doubled(gram, got, distance, me)
    apart = [x.reshape(count // 2, -1, BLOCK) for x in (gram, got)]
    notes = jnp.concatenate([x[:, shard] for x in apart], axis=0)
    gram, got = [x[:, :shard].reshape(-1, BLOCK) for x in apart]
    gram = doubled(gram, got, 1, me)

    weight, inverse = poly_pass(notes, gram, latent)

    column = me * column_count + jnp.arange(column_count, dtype=jnp.int32)
    after = jnp.concatenate([offsets[1:], jnp.full((1,), out_total, offsets.dtype)])
    inside = (column[None, :] >= offsets[:, None]) & (column[None, :] < after[:, None])
    column_scale = jnp.sum(jnp.where(inside, target_scale[:, None], 0.0), axis=0, keepdims=True)
    scale = column_scale * math.sqrt(out_total)
    step = step_pass(weight, inverse, scale, momentum, columns)
    return new_momentum, step


def solution(mesh):
    split = P(None, AXES)

    def whole(factor_grads, latents, task_ids, offsets, target_scale, momentum):
        return jax.shard_map(
            functools.partial(per_device, momentum.shape[1]),
            mesh=mesh,
            in_specs=(P(AXES, None), P(AXES, None), P(AXES), P(), P(), split),
            out_specs=(split, split),
            check_vma=False,
        )(factor_grads, latents, task_ids, offsets, target_scale, momentum)

    return whole
```

time: 881 us -> 168 us (0.19)
  waiting for transfers between devices: 394 us -> 28.8 us
  matrix products: 316 us -> 0.28 us
  blocking collectives: 142 us -> 0 us
  Pallas kernels: 0 us -> 86.6 us
  starting transfers between devices: 7.64 us -> 32.1 us
  between operations: 14.7 us -> 1.13 us
  local copies, waits for them, and re-layouts: 2.18 us -> 11.9 us
    dot_general x7 -> x1, matrix products: 316 us -> 0.28 us  [dot(): return jnp.dot(a, b, preferred_element_type=F32)]
    psum x2 -> x0, waiting for transfers between devices: 283 us -> none  [summed_gram(): return lax.psum(partial_gram, ('gx', 'gy'))]
    all_gather x2 -> x0, waiting for transfers between devices: 110 us -> none  [per_device(): lax.all_gather(poly_rows.astype(jnp.bfloat16), ('gx', 'gy'), axis=0, tile...]
    pallas_call x0 -> x13, Pallas kernels: none -> 86.6 us  [the longest x1 24.4 us: step_pass(): pl.pallas_call(step_kernel, grid=(count // tile,), in_specs=[pl.BlockSpec...]
    all_gather x1 -> x0, blocking collectives: 61.6 us -> none  [per_device(): lax.all_gather(latents, ('gx', 'gy'), axis=0, tiled=True)]
    unnamed x1 -> x0, blocking collectives: 40.4 us -> none
    psum x1 -> x0, blocking collectives: 39.7 us -> none  [per_device(): squares = lax.psum(jnp.sum(blended * blended), ('gx', 'gy'))]
    ppermute x0 -> x15, waiting for transfers between devices: none -> 28.8 us  [swap(): return lax.ppermute(x, AXES, [(i, i ^ distance) for i in range(count)])]
  transfers between devices with their start and end apart: 5 -> 16, of which waited for: 4 -> 11; matrix products, arithmetic and copies ran while one was open for 0% -> 3% of each run, Pallas kernels for 0% -> 28%
where the time goes in v1:
time: 168 us; the launch traced here: 167 us
  Pallas kernels  86.6 us (52%)
  starting transfers between devices  32.1 us (19%)
  waiting for transfers between devices  28.8 us (17%)
  local copies, waits for them, and re-layouts  11.9 us (7%)
  other arithmetic  6.43 us (4%)
    ppermute x15, waiting for transfers between devices, swap(): return lax.ppermute(x, AXES, [(i, i ^ distance) for i in range(count)])  28.8 us
    ppermute x15, starting transfers between devices, swap(): return lax.ppermute(x, AXES, [(i, i ^ distance) for i in range(count)])  24.8 us
    pallas_call x1, Pallas kernels, step_pass(): pl.pallas_call(step_kernel, grid=(count // tile,), in_specs=[pl.BlockSpec...  24.4 us
    pallas_call x3, Pallas kernels, momentum_piece(): pl.pallas_call(momentum_kernel, grid=(steps,), in_specs=[pl.BlockSpec((ta...  19.3 us
    pallas_call x1, Pallas kernels, gram_pass(): pl.pallas_call(gram_kernel, grid=(count // tile,), in_specs=[pl.BlockSpec...  18.8 us
    pallas_call x1, Pallas kernels, poly_pass(): pl.pallas_call(poly_kernel, in_specs=[whole, whole, whole], out_specs=[wh...  13.8 us
    pallas_call x1, Pallas kernels, cross_pass(): pl.pallas_call(cross_kernel, grid=(count // tile,), in_specs=[pl.BlockSpe...  9 us
    all_to_all x1, starting transfers between devices, per_device(): lax.all_to_all(factor_grads, AXES, split_axis=1, concat_axis=0, tiled=True)  7.3 us
  transfers between devices with their start and end apart: 16, of which 11 were waited for; matrix products, arithmetic and copies ran while one was open for 3% of the time, Pallas kernels for 28%

profile of v1, /device:TPU:0, one launch (start us, length us, event | category | flops | bytes accessed | tf_op | source)
XLA Modules:
  0.0 167.2 jit_solution(16632564587097528366)
XLA Ops:
  0.6 7.3 %all-to-all-start = ((bf16[4,32,6144]{2,0,1:T(4,128)(2,1)}), bf16[4,32,6144]{2,0,1:T(4,128)(2,1)S(1)}, u32[]{:S(2)}, u32[]{:S(2)}) async-start(bf16[4,32,6144]{2,0,1:T(4,128)(2,1)} %bitcast.22), calls=%async_computation | async-start | bytes 3145728 | tf_op jit(solution)/shard_map/all_to_all | solution.py:392
  8.0 0.1 copy.25
  8.1 0.1 copy.26
  8.2 0.1 fusion.6
  8.3 0.3 collective-permute-start
  8.6 0.9 collective-permute-done
  9.6 1.8 %collective-permute-start.1 = (bf16[8,1152]{1,0:T(8,128)(2,1)S(1)}, bf16[8,1152]{1,0:T(8,128)(2,1)S(1)}, u32[]{:S(2)}, u32[]{:S(2)}) collective-permute-start(bf16[8,1152]{1,0:T(8,128)(2,1)S(1)} %pad_maximum_fusion.8), channel_id=1, source_target_pairs={{0,2},{1,3},{2,0},{3,1},{4,6},{5,7},{6,4},{7,5},{8,10},{9,11},{10,... | collective-permute-start | bytes 55304 | tf_op jit(solution)/shard_map/ppermute | solution.py:36
  11.4 2.6 %collective-permute-done.1 = bf16[8,1152]{1,0:T(8,128)(2,1)S(1)} collective-permute-done((bf16[8,1152]{1,0:T(8,128)(2,1)S(1)}, bf16[8,1152]{1,0:T(8,128)(2,1)S(1)}, u32[]{:S(2)}, u32[]{:S(2)}) %collective-permute-start.1) | collective-permute-done | bytes 18464 | tf_op jit(solution)/shard_map/ppermute | solution.py:36
  14.0 6.3 %collective-permute-start.2 = (bf16[16,1152]{1,0:T(8,128)(2,1)S(1)}, bf16[16,1152]{1,0:T(8,128)(2,1)S(1)}, u32[]{:S(2)}, u32[]{:S(2)}) collective-permute-start(bf16[16,1152]{1,0:T(8,128)(2,1)S(1)} %pad_maximum_fusion.7), channel_id=1, source_target_pairs={{0,4},{1,5},{2,6},{3,7},{4,0},{5,1},{6,2},{7,3},{8,12},{9,13},{10,... | collective-permute-start | bytes 110600 | tf_op jit(solution)/shard_map/ppermute | solution.py:36
  20.4 18.8 %momentum_gram.1 = (bf16[1024,6144]{1,0:T(8,128)(2,1)}, f32[2560,256]{1,0:T(8,128)}, f32[8,128]{1,0:T(8,128)}) custom-call(f32[1024,6144]{1,0:T(8,128)} %momentum_ref.9), custom_call_target="tpu_custom_call" | custom-call | flops 1 | bytes 1 | tf_op jit(solution)/shard_map/momentum_gram/pallas_call | solution.py:110
  39.2 0.1 collective-permute-start.3
  39.3 6.4 %collective-permute-done.3.x_ref = bf16[32,1152]{1,0:T(8,128)(2,1)S(1)} collective-permute-done((bf16[32,1152]{1,0:T(8,128)(2,1)S(1)}, bf16[32,1152]{1,0:T(8,128)(2,1)S(1)}, u32[]{:S(2)}, u32[]{:S(2)}) %collective-permute-start.3) | collective-permute-done | bytes 73760 | tf_op jit(solution)/shard_map/ppermute | solution.py:36
  45.7 0.6 copy-done.11
  46.4 3.4 %concatenate.50 = bf16[64,1152]{1,0:T(8,128)(2,1)} concatenate(bf16[4,1152]{1,0:T(4,128)(2,1)S(1)} %pad_maximum_fusion.10, bf16[4,1152]{1,0:T(4,128)(2,1)S(1)} %collective-permute-done, bf16[8,1152]{1,0:T(8,128)(2,1)S(1)} %collective-permute-done.1, bf16[16,1152]{1,0:T(8,128)(2,1)S(1)} %collective-permute-done.2, bf16[32,1152]{1,0:T(8,128)(2,1)} %tie.5), dimensions={0} | concatenate | bytes 294912 | tf_op jit(solution)/shard_map/concatenate | solution.py:402
  49.8 1.4 all_to_all.17.columns_ref
  51.2 9.0 %cross_terms.1.after_ref.cross_ref = f32[128,1152]{1,0:T(8,128)} custom-call(bf16[128,6144]{1,0:T(8,128)(2,1)} %all_to_all.17.columns_ref, bf16[1024,6144]{1,0:T(8,128)(2,1)} %get-tuple-element.17.rounded_ref), custom_call_target="tpu_custom_call" | custom-call | flops 1610612736 | bytes 12582912 | tf_op jit(solution)/shard_map/cross_terms/pallas_call | solution.py:147
  60.2 1.0 concatenate.51
  61.2 0.2 add_reduce_fusion
  61.4 0.1 select_reduce_fusion.1
  61.5 0.3 convolution_convert_fusion.latent_ref
  61.9 1.1 copy-done.3
  63.0 1.3 blended_gram.1
  64.3 0.0 copy-start.5
  64.3 1.0 copy-done.5
  65.4 2.1 %collective-permute-done.5 = bf16[1280,256]{1,0:T(8,128)(2,1)S(1)} collective-permute-done((bf16[1280,256]{1,0:T(8,128)(2,1)S(1)}, bf16[1280,256]{1,0:T(8,128)(2,1)S(1)}, u32[]{:S(2)}, u32[]{:S(2)}) %collective-permute-start.5) | collective-permute-done | bytes 655392 | tf_op jit(solution)/shard_map/ppermute | solution.py:36
  67.5 1.5 convert_add_fusion
  69.1 0.0 copy-start.10
  69.1 2.0 %collective-permute-start.6 = (bf16[640,256]{1,0:T(8,128)(2,1)S(1)}, bf16[640,256]{1,0:T(8,128)(2,1)S(1)}, u32[]{:S(2)}, u32[]{:S(2)}) collective-permute-start(bf16[640,256]{1,0:T(8,128)(2,1)S(1)} %dynamic-slice_convert_fusion.refs_0_), channel_id=1, source_target_pairs={{0,2},{1,3},{2,0},{3,1},{4,6},{5,7},{6,4},{7,5},{8,10},{9,11},{10,... | collective-permute-start | bytes 983048 | tf_op jit(solution)/shard_map/ppermute | solution.py:36
  71.1 6.5 %new_momentum.3 = (f32[1024,6144]{1,0:T(8,128)}, f32[8,128]{1,0:T(8,128)}) custom-call(bf16[128,1024]{1,0:T(8,128)(2,1)} %copy-done.1, f32[1024,6144]{1,0:T(8,128)} %momentum_ref.9, bf16[128,6144]{1,0:T(8,128)(2,1)} %all_to_all.17.columns_ref, bf16[640,256]{1,0:T(8,128)(2,1)} %copy-done.10), custom_call_target="tpu_custom_call" | custom-call | flops 1 | bytes 1 | tf_op jit(solution)/shard_map/new_momentum/pallas_call | solution.py:238
  77.5 1.5 collective-permute-done.6.x_ref
  79.1 0.7 copy-done.9
  79.8 1.0 convert_add_fusion.1
  80.9 0.0 copy-start.14
  80.9 0.9 collective-permute-start.7
  81.8 6.4 %new_momentum.4 = (f32[1024,6144]{1,0:T(8,128)}, f32[8,128]{1,0:T(8,128)}) custom-call(bf16[128,1024]{1,0:T(8,128)(2,1)} %copy-done.1, f32[1024,6144]{1,0:T(8,128)} %momentum_ref.9, bf16[128,6144]{1,0:T(8,128)(2,1)} %all_to_all.17.columns_ref, bf16[320,256]{1,0:T(8,128)(2,1)} %copy-done.14, ...), custom_call_target="tpu_custom_call", output_to_operand_aliasing={{0}: (4, {})} | custom-call | flops 1 | bytes 1 | tf_op jit(solution)/shard_map/new_momentum/pallas_call | solution.py:238
  88.2 0.7 copy-done.13
  88.9 0.9 convert_add_fusion.2
  89.9 1.9 %collective-permute-start.8 = (bf16[160,256]{1,0:T(8,128)(2,1)S(1)}, bf16[160,256]{1,0:T(8,128)(2,1)S(1)}, u32[]{:S(2)}, u32[]{:S(2)}) collective-permute-start(bf16[160,256]{1,0:T(8,128)(2,1)S(1)} %dynamic-slice_convert_fusion.2), channel_id=1, source_target_pairs={{0,8},{1,9},{2,10},{3,11},{4,12},{5,13},{6,14},{7,15},{8,0},{9,1},... | collective-permute-start | bytes 245768 | tf_op jit(solution)/shard_map/ppermute | solution.py:36
  91.7 2.6 %collective-permute-done.8 = bf16[160,256]{1,0:T(8,128)(2,1)S(1)} collective-permute-done((bf16[160,256]{1,0:T(8,128)(2,1)S(1)}, bf16[160,256]{1,0:T(8,128)(2,1)S(1)}, u32[]{:S(2)}, u32[]{:S(2)}) %collective-permute-start.8) | collective-permute-done | bytes 81952 | tf_op jit(solution)/shard_map/ppermute | solution.py:36
  94.4 2.7 %collective-permute-start.9 = (bf16[80,256]{1,0:T(8,128)(2,1)S(1)}, bf16[80,256]{1,0:T(8,128)(2,1)S(1)}, u32[]{:S(2)}, u32[]{:S(2)}) collective-permute-start(bf16[80,256]{1,0:T(8,128)(2,1)S(1)} %dynamic-slice_convert_fusion.3), channel_id=1, source_target_pairs={{0,16},{1,17},{2,18},{3,19},{4,20},{5,21},{6,22},{7,23},{8,24},{9,... | collective-permute-start | bytes 122888 | tf_op jit(solution)/shard_map/ppermute | solution.py:36
  97.1 2.2 %collective-permute-done.9 = bf16[80,256]{1,0:T(8,128)(2,1)S(1)} collective-permute-done((bf16[80,256]{1,0:T(8,128)(2,1)S(1)}, bf16[80,256]{1,0:T(8,128)(2,1)S(1)}, u32[]{:S(2)}, u32[]{:S(2)}) %collective-permute-start.9) | collective-permute-done | bytes 40992 | tf_op jit(solution)/shard_map/ppermute | solution.py:36
  99.4 2.8 %collective-permute-start.10 = (bf16[96,256]{1,0:T(8,128)(2,1)S(1)}, bf16[96,256]{1,0:T(8,128)(2,1)S(1)}, u32[]{:S(2)}, u32[]{:S(2)}) collective-permute-start(bf16[96,256]{1,0:T(8,128)(2,1)S(1)} %pad_maximum_fusion.6), channel_id=1, source_target_pairs={{0,16},{1,17},{2,18},{3,19},{4,20},{5,21},{6,22},{7,23},{8,24},{9,... | collective-permute-start | bytes 147464 | tf_op jit(solution)/shard_map/ppermute | solution.py:36
  102.2 2.4 %collective-permute-done.10 = bf16[96,256]{1,0:T(8,128)(2,1)S(1)} collective-permute-done((bf16[96,256]{1,0:T(8,128)(2,1)S(1)}, bf16[96,256]{1,0:T(8,128)(2,1)S(1)}, u32[]{:S(2)}, u32[]{:S(2)}) %collective-permute-start.10) | collective-permute-done | bytes 49184 | tf_op jit(solution)/shard_map/ppermute | solution.py:36
  104.6 2.2 %collective-permute-start.11 = (bf16[192,256]{1,0:T(8,128)(2,1)S(1)}, bf16[192,256]{1,0:T(8,128)(2,1)S(1)}, u32[]{:S(2)}, u32[]{:S(2)}) collective-permute-start(bf16[192,256]{1,0:T(8,128)(2,1)S(1)} %pad_maximum_fusion.4), channel_id=1, source_target_pairs={{0,8},{1,9},{2,10},{3,11},{4,12},{5,13},{6,14},{7,15},{8,0},{9,1},... | collective-permute-start | bytes 294920 | tf_op jit(solution)/shard_map/ppermute | solution.py:36
  106.8 2.6 %collective-permute-done.11 = bf16[192,256]{1,0:T(8,128)(2,1)S(1)} collective-permute-done((bf16[192,256]{1,0:T(8,128)(2,1)S(1)}, bf16[192,256]{1,0:T(8,128)(2,1)S(1)}, u32[]{:S(2)}, u32[]{:S(2)}) %collective-permute-start.11) | collective-permute-done | bytes 98336 | tf_op jit(solution)/shard_map/ppermute | solution.py:36
  109.5 1.7 collective-permute-start.12
  111.2 4.1 %collective-permute-done.12 = bf16[384,256]{1,0:T(8,128)(2,1)S(1)} collective-permute-done((bf16[384,256]{1,0:T(8,128)(2,1)S(1)}, bf16[384,256]{1,0:T(8,128)(2,1)S(1)}, u32[]{:S(2)}, u32[]{:S(2)}) %collective-permute-start.12) | collective-permute-done | bytes 196640 | tf_op jit(solution)/shard_map/ppermute | solution.py:36
  115.2 0.1 broadcast_select_fusion.5
  115.4 2.0 %collective-permute-start.13 = (bf16[768,256]{1,0:T(8,128)(2,1)S(1)}, bf16[768,256]{1,0:T(8,128)(2,1)S(1)}, u32[]{:S(2)}, u32[]{:S(2)}) collective-permute-start(bf16[768,256]{1,0:T(8,128)(2,1)S(1)} %pad_maximum_fusion.2.refs_0_), channel_id=1, source_target_pairs={{0,2},{1,3},{2,0},{3,1},{4,6},{5,7},{6,4},{7,5},{8,10},{9,11},{10,... | collective-permute-start | bytes 1179656 | tf_op jit(solution)/shard_map/ppermute | solution.py:36
  117.3 6.4 %new_momentum.5 = (f32[1024,6144]{1,0:T(8,128)}, f32[8,128]{1,0:T(8,128)}) custom-call(bf16[128,1024]{1,0:T(8,128)(2,1)} %copy-done.1, f32[1024,6144]{1,0:T(8,128)} %momentum_ref.9, bf16[128,6144]{1,0:T(8,128)(2,1)} %all_to_all.17.columns_ref, bf16[768,256]{1,0:T(8,128)(2,1)} %copy-done.7, ...), custom_call_target="tpu_custom_call", output_to_operand_aliasing={{0}: (4, {})} | custom-call | flops 1 | bytes 1 | tf_op jit(solution)/shard_map/new_momentum/pallas_call | solution.py:238
  123.8 0.0 copy-start.8
  123.8 0.7 copy-done.8
  124.5 1.2 broadcast_select_fusion.3
  125.7 0.1 pad_maximum_fusion.1
  125.8 0.1 collective-permute-start.14
  125.8 0.1 slice.31
  125.9 0.1 pad_add_fusion
  126.0 0.8 select_reduce_fusion
  126.8 1.3 collective-permute-done.14
  128.1 0.1 broadcast_select_fusion.1
  128.3 0.1 pad_maximum_fusion.gram_ref
  128.4 0.7 copy-done.2
  129.1 13.8 %polynomial.1 = (bf16[1024,1280]{1,0:T(8,128)(2,1)}, f32[8,128]{1,0:T(8,128)S(1)}) custom-call(bf16[32,256]{1,0:T(8,128)(2,1)S(1)} %pad_maximum_fusion.9.notes_ref, bf16[2560,256]{1,0:T(8,128)(2,1)S(1)} %pad_maximum_fusion.gram_ref, bf16[128,1024]{1,0:T(8,128)(2,1)S(1)} %copy-done.2), custom_call_target="tpu_custom_call" | custom-call | flops 10737418240 | bytes 4194304 | tf_op jit(solution)/shard_map/polynomial/pallas_call | solution.py:312
  142.8 24.4 %step.1 = f32[1024,6144]{1,0:T(8,128)} custom-call(bf16[1024,1280]{1,0:T(8,128)(2,1)} %get-tuple-element.28.weight_ref, f32[8,128]{1,0:T(8,128)S(1)} %get-tuple-element.29.inverse_ref, f32[1,6144]{1,0:T(1,128)S(1)} %bitcast.16, f32[1024,6144]{1,0:T(8,128)} %momentum_ref.9, bf16[128,6144]{1,0:T(8,128)(2,1)S(1)} %copy-done), custom_call_target="tpu_custom_call" | custom-call | flops 16106127360 | bytes 50331648 | tf_op jit(solution)/shard_map/step/pallas_call | solution.py:350
  (79 shorter events, 0.5 us)
Async XLA Ops:
  0.6 7.3 %copy-start.26 = (s32[4]{0:T(128)S(1)}, s32[4]{0:T(128)}, u32[]{:S(2)}) copy-start(s32[4]{0:T(128)} %param.8) | copy-start | bytes 52
  0.6 7.6 %copy-start.21 = (bf16[4,1024]{1,0:T(4,128)(2,1)S(1)}, bf16[4,1024]{1,0:T(4,128)(2,1)}, u32[]{:S(2)}) copy-start(bf16[4,1024]{1,0:T(4,128)(2,1)} %param.7) | copy-start | bytes 24580
  0.6 49.1 %all-to-all-start = ((bf16[4,32,6144]{2,0,1:T(4,128)(2,1)}), bf16[4,32,6144]{2,0,1:T(4,128)(2,1)S(1)}, u32[]{:S(2)}, u32[]{:S(2)}) async-start(bf16[4,32,6144]{2,0,1:T(4,128)(2,1)} %bitcast.22), calls=%async_computation | async-start | bytes 3145728 | tf_op jit(solution)/shard_map/all_to_all | solution.py:392
  8.3 38.1 %copy-start.22 = (bf16[4,1152]{1,0:T(4,128)(2,1)}, bf16[4,1152]{1,0:T(4,128)(2,1)S(1)}, u32[]{:S(2)}) copy-start(bf16[4,1152]{1,0:T(4,128)(2,1)S(1)} %pad_maximum_fusion.10) | copy-start | bytes 27652
  8.3 1.2 collective-permute-start
  9.5 36.8 %copy-start.19 = (bf16[4,1152]{1,0:T(4,128)(2,1)}, bf16[4,1152]{1,0:T(4,128)(2,1)S(1)}, u32[]{:S(2)}) copy-start(bf16[4,1152]{1,0:T(4,128)(2,1)S(1)} %collective-permute-done) | copy-start | bytes 27652
  9.6 4.4 %collective-permute-start.1 = (bf16[8,1152]{1,0:T(8,128)(2,1)S(1)}, bf16[8,1152]{1,0:T(8,128)(2,1)S(1)}, u32[]{:S(2)}, u32[]{:S(2)}) collective-permute-start(bf16[8,1152]{1,0:T(8,128)(2,1)S(1)} %pad_maximum_fusion.8), channel_id=1, source_target_pairs={{0,2},{1,3},{2,0},{3,1},{4,6},{5,7},{6,4},{7,5},{8,10},{9,11},{10,... | collective-permute-start | bytes 55304 | tf_op jit(solution)/shard_map/ppermute | solution.py:36
  14.0 32.4 %copy-start.17 = (bf16[8,1152]{1,0:T(8,128)(2,1)}, bf16[8,1152]{1,0:T(8,128)(2,1)S(1)}, u32[]{:S(2)}) copy-start(bf16[8,1152]{1,0:T(8,128)(2,1)S(1)} %collective-permute-done.1) | copy-start | bytes 55300
  14.0 25.2 %collective-permute-start.2 = (bf16[16,1152]{1,0:T(8,128)(2,1)S(1)}, bf16[16,1152]{1,0:T(8,128)(2,1)S(1)}, u32[]{:S(2)}, u32[]{:S(2)}) collective-permute-start(bf16[16,1152]{1,0:T(8,128)(2,1)S(1)} %pad_maximum_fusion.7), channel_id=1, source_target_pairs={{0,4},{1,5},{2,6},{3,7},{4,0},{5,1},{6,2},{7,3},{8,12},{9,13},{10,... | collective-permute-start | bytes 110600 | tf_op jit(solution)/shard_map/ppermute | solution.py:36
  39.2 11.9 %copy-start.15 = (bf16[16,1152]{1,0:T(8,128)(2,1)}, bf16[16,1152]{1,0:T(8,128)(2,1)S(1)}, u32[]{:S(2)}) copy-start(bf16[16,1152]{1,0:T(8,128)(2,1)S(1)} %collective-permute-done.2) | copy-start | bytes 110596
  39.2 6.5 %collective-permute-start.3 = (bf16[32,1152]{1,0:T(8,128)(2,1)S(1)}, bf16[32,1152]{1,0:T(8,128)(2,1)S(1)}, u32[]{:S(2)}, u32[]{:S(2)}) collective-permute-start(bf16[32,1152]{1,0:T(8,128)(2,1)S(1)} %pad_maximum_fusion.5), channel_id=1, source_target_pairs={{0,8},{1,9},{2,10},{3,11},{4,12},{5,13},{6,14},{7,15},{8,0},{9,1},... | collective-permute-start | bytes 221192 | tf_op jit(solution)/shard_map/ppermute | solution.py:36
  45.7 0.6 copy-start.11
  49.7 10.4 %collective-permute-start.4 = (bf16[64,1152]{1,0:T(8,128)(2,1)}, bf16[64,1152]{1,0:T(8,128)(2,1)}, u32[]{:S(2)}, u32[]{:S(2)}) collective-permute-start(bf16[64,1152]{1,0:T(8,128)(2,1)} %concatenate.50), channel_id=1, source_target_pairs={{0,16},{1,17},{2,18},{3,19},{4,20},{5,21},{6,22},{7,23},{8,24},{9,... | collective-permute-start | bytes 442376 | tf_op jit(solution)/shard_map/ppermute | solution.py:36
  51.1 9.1 %copy-start.12 = (bf16[32,1152]{1,0:T(8,128)(2,1)S(1)}, bf16[32,1152]{1,0:T(8,128)(2,1)}, u32[]{:S(2)}) copy-start(bf16[32,1152]{1,0:T(8,128)(2,1)} %tie.5) | copy-start | bytes 221188
  51.1 9.1 %copy-start.16 = (bf16[16,1152]{1,0:T(8,128)(2,1)S(1)}, bf16[16,1152]{1,0:T(8,128)(2,1)}, u32[]{:S(2)}) copy-start(bf16[16,1152]{1,0:T(8,128)(2,1)} %copy-done.15) | copy-start | bytes 110596
  51.1 9.1 %copy-start.18 = (bf16[8,1152]{1,0:T(8,128)(2,1)S(1)}, bf16[8,1152]{1,0:T(8,128)(2,1)}, u32[]{:S(2)}) copy-start(bf16[8,1152]{1,0:T(8,128)(2,1)} %copy-done.17) | copy-start | bytes 55300
  51.1 9.1 %copy-start.20 = (bf16[4,1152]{1,0:T(4,128)(2,1)S(1)}, bf16[4,1152]{1,0:T(4,128)(2,1)}, u32[]{:S(2)}) copy-start(bf16[4,1152]{1,0:T(4,128)(2,1)} %copy-done.19) | copy-start | bytes 27652
  51.1 9.1 %copy-start.23 = (bf16[4,1152]{1,0:T(4,128)(2,1)S(1)}, bf16[4,1152]{1,0:T(4,128)(2,1)}, u32[]{:S(2)}) copy-start(bf16[4,1152]{1,0:T(4,128)(2,1)} %copy-done.22) | copy-start | bytes 27652
  51.1 10.7 %copy-start.4 = (f32[2560,256]{1,0:T(8,128)S(1)}, f32[2560,256]{1,0:T(8,128)}, u32[]{:S(2)}) copy-start(f32[2560,256]{1,0:T(8,128)} %get-tuple-element.18.momentum_gram_ref) | copy-start | bytes 7864324
  51.1 10.7 %copy-start.6 = (f32[8,128]{1,0:T(8,128)S(1)}, f32[8,128]{1,0:T(8,128)}, u32[]{:S(2)}) copy-start(f32[8,128]{1,0:T(8,128)} %get-tuple-element.16.after_ref.squares_ref) | copy-start | bytes 12292
  61.8 7.2 %copy-start.1 = (bf16[128,1024]{1,0:T(8,128)(2,1)}, bf16[128,1024]{1,0:T(8,128)(2,1)S(1)}, u32[]{:S(2)}) copy-start(bf16[128,1024]{1,0:T(8,128)(2,1)S(1)} %convolution_convert_fusion.latent_ref) | copy-start | bytes 786436
  61.9 1.1 copy-start.3
  64.3 1.1 copy-start.5
  65.4 2.1 %collective-permute-start.5 = (bf16[1280,256]{1,0:T(8,128)(2,1)S(1)}, bf16[1280,256]{1,0:T(8,128)(2,1)S(1)}, u32[]{:S(2)}, u32[]{:S(2)}) collective-permute-start(bf16[1280,256]{1,0:T(8,128)(2,1)S(1)} %get-tuple-element.20), channel_id=1, source_target_pairs={{0,1},{1,0},{2,3},{3,2},{4,5},{5,4},{6,7},{7,6},{8,9},{9,8},{10,11... | collective-permute-start | bytes 1966088 | tf_op jit(solution)/shard_map/ppermute | solution.py:36
  69.1 2.0 %copy-start.10 = (bf16[640,256]{1,0:T(8,128)(2,1)}, bf16[640,256]{1,0:T(8,128)(2,1)S(1)}, u32[]{:S(2)}) copy-start(bf16[640,256]{1,0:T(8,128)(2,1)S(1)} %dynamic-slice_convert_fusion.refs_0_) | copy-start | bytes 983044
  69.1 10.0 %collective-permute-start.6 = (bf16[640,256]{1,0:T(8,128)(2,1)S(1)}, bf16[640,256]{1,0:T(8,128)(2,1)S(1)}, u32[]{:S(2)}, u32[]{:S(2)}) collective-permute-start(bf16[640,256]{1,0:T(8,128)(2,1)S(1)} %dynamic-slice_convert_fusion.refs_0_), channel_id=1, source_target_pairs={{0,2},{1,3},{2,0},{3,1},{4,6},{5,7},{6,4},{7,5},{8,10},{9,11},{10,... | collective-permute-start | bytes 983048 | tf_op jit(solution)/shard_map/ppermute | solution.py:36
  79.1 0.7 copy-start.9
  80.9 0.9 copy-start.14
  80.9 7.3 %collective-permute-start.7 = (bf16[320,256]{1,0:T(8,128)(2,1)S(1)}, bf16[320,256]{1,0:T(8,128)(2,1)S(1)}, u32[]{:S(2)}, u32[]{:S(2)}) collective-permute-start(bf16[320,256]{1,0:T(8,128)(2,1)S(1)} %dynamic-slice_convert_fusion.1.refs_0_), channel_id=1, source_target_pairs={{0,4},{1,5},{2,6},{3,7},{4,0},{5,1},{6,2},{7,3},{8,12},{9,13},{10,... | collective-permute-start | bytes 491528 | tf_op jit(solution)/shard_map/ppermute | solution.py:36
  88.2 0.7 copy-start.13
  89.9 4.5 %collective-permute-start.8 = (bf16[160,256]{1,0:T(8,128)(2,1)S(1)}, bf16[160,256]{1,0:T(8,128)(2,1)S(1)}, u32[]{:S(2)}, u32[]{:S(2)}) collective-permute-start(bf16[160,256]{1,0:T(8,128)(2,1)S(1)} %dynamic-slice_convert_fusion.2), channel_id=1, source_target_pairs={{0,8},{1,9},{2,10},{3,11},{4,12},{5,13},{6,14},{7,15},{8,0},{9,1},... | collective-permute-start | bytes 245768 | tf_op jit(solution)/shard_map/ppermute | solution.py:36
  94.4 5.0 %collective-permute-start.9 = (bf16[80,256]{1,0:T(8,128)(2,1)S(1)}, bf16[80,256]{1,0:T(8,128)(2,1)S(1)}, u32[]{:S(2)}, u32[]{:S(2)}) collective-permute-start(bf16[80,256]{1,0:T(8,128)(2,1)S(1)} %dynamic-slice_convert_fusion.3), channel_id=1, source_target_pairs={{0,16},{1,17},{2,18},{3,19},{4,20},{5,21},{6,22},{7,23},{8,24},{9,... | collective-permute-start | bytes 122888 | tf_op jit(solution)/shard_map/ppermute | solution.py:36
  99.4 5.2 %collective-permute-start.10 = (bf16[96,256]{1,0:T(8,128)(2,1)S(1)}, bf16[96,256]{1,0:T(8,128)(2,1)S(1)}, u32[]{:S(2)}, u32[]{:S(2)}) collective-permute-start(bf16[96,256]{1,0:T(8,128)(2,1)S(1)} %pad_maximum_fusion.6), channel_id=1, source_target_pairs={{0,16},{1,17},{2,18},{3,19},{4,20},{5,21},{6,22},{7,23},{8,24},{9,... | collective-permute-start | bytes 147464 | tf_op jit(solution)/shard_map/ppermute | solution.py:36
  104.6 4.8 %collective-permute-start.11 = (bf16[192,256]{1,0:T(8,128)(2,1)S(1)}, bf16[192,256]{1,0:T(8,128)(2,1)S(1)}, u32[]{:S(2)}, u32[]{:S(2)}) collective-permute-start(bf16[192,256]{1,0:T(8,128)(2,1)S(1)} %pad_maximum_fusion.4), channel_id=1, source_target_pairs={{0,8},{1,9},{2,10},{3,11},{4,12},{5,13},{6,14},{7,15},{8,0},{9,1},... | collective-permute-start | bytes 294920 | tf_op jit(solution)/shard_map/ppermute | solution.py:36
  109.5 5.7 %collective-permute-start.12 = (bf16[384,256]{1,0:T(8,128)(2,1)S(1)}, bf16[384,256]{1,0:T(8,128)(2,1)S(1)}, u32[]{:S(2)}, u32[]{:S(2)}) collective-permute-start(bf16[384,256]{1,0:T(8,128)(2,1)S(1)} %pad_maximum_fusion.3), channel_id=1, source_target_pairs={{0,4},{1,5},{2,6},{3,7},{4,0},{5,1},{6,2},{7,3},{8,12},{9,13},{10,... | collective-permute-start | bytes 589832 | tf_op jit(solution)/shard_map/ppermute | solution.py:36
  115.3 2.0 %copy-start.7 = (bf16[768,256]{1,0:T(8,128)(2,1)}, bf16[768,256]{1,0:T(8,128)(2,1)S(1)}, u32[]{:S(2)}) copy-start(bf16[768,256]{1,0:T(8,128)(2,1)S(1)} %pad_maximum_fusion.2.refs_0_) | copy-start | bytes 1179652
  115.4 8.4 %collective-permute-start.13 = (bf16[768,256]{1,0:T(8,128)(2,1)S(1)}, bf16[768,256]{1,0:T(8,128)(2,1)S(1)}, u32[]{:S(2)}, u32[]{:S(2)}) collective-permute-start(bf16[768,256]{1,0:T(8,128)(2,1)S(1)} %pad_maximum_fusion.2.refs_0_), channel_id=1, source_target_pairs={{0,2},{1,3},{2,0},{3,1},{4,6},{5,7},{6,4},{7,5},{8,10},{9,11},{10,... | collective-permute-start | bytes 1179656 | tf_op jit(solution)/shard_map/ppermute | solution.py:36
  123.8 2.1 %copy-start.24 = (s32[160]{0:T(256)S(1)}, s32[160]{0:T(256)}, u32[]{:S(2)}) copy-start(s32[160]{0:T(256)} %param.9) | copy-start | bytes 1924
  123.8 2.2 %copy-start.25 = (f32[160]{0:T(256)S(1)}, f32[160]{0:T(256)}, u32[]{:S(2)}) copy-start(f32[160]{0:T(256)} %param.10) | copy-start | bytes 1924
  123.8 0.7 copy-start.8
  125.8 2.4 %collective-permute-start.14 = (bf16[1536,256]{1,0:T(8,128)(2,1)S(1)}, bf16[1536,256]{1,0:T(8,128)(2,1)S(1)}, u32[]{:S(2)}, u32[]{:S(2)}) collective-permute-start(bf16[1536,256]{1,0:T(8,128)(2,1)S(1)} %pad_maximum_fusion.1), channel_id=1, source_target_pairs={{0,1},{1,0},{2,3},{3,2},{4,5},{5,4},{6,7},{7,6},{8,9},{9,8},{10,11... | collective-permute-start | bytes 2359304 | tf_op jit(solution)/shard_map/ppermute | solution.py:36
  128.1 1.0 copy-start.2
  129.1 13.8 %copy-start = (bf16[128,6144]{1,0:T(8,128)(2,1)S(1)}, bf16[128,6144]{1,0:T(8,128)(2,1)}, u32[]{:S(2)}) copy-start(bf16[128,6144]{1,0:T(8,128)(2,1)} %all_to_all.17.columns_ref) | copy-start | bytes 4718596

commit v2 on v1

--- a/solution.py
+++ b/solution.py
@@ -49,31 +49,8 @@
     return jnp.concatenate([latents, jnp.pad(id_columns, ((0, 0), (0, LANES - 2)))], axis=1)
 
 
-def chosen_latents(held, me, rows, width):
-    tasks = held.shape[0]
-    place = jnp.arange(tasks, dtype=jnp.int32)
-    origin = ((place // rows) ^ me) * rows + place % rows
-    held_ids = held[:, width].astype(jnp.int32) * 256 + held[:, width + 1].astype(jnp.int32)
-    ids = jnp.sum(jnp.where(origin[None, :] == place[:, None], held_ids[None, :], 0), axis=1)
-    chosen = (ids[:, None] == origin[None, :]).astype(BF16)
-    return dot(chosen, held[:, :width]).astype(BF16)
-
-
-def tie_kernel(x_ref, after_ref, out_ref):
-    del x_ref, after_ref, out_ref
-
-
-def tied(x, after):
-    anywhere = pl.BlockSpec(memory_space=pl.ANY)
-    return pl.pallas_call(
-        tie_kernel,
-        in_specs=[anywhere, anywhere],
-        out_specs=anywhere,
-        out_shape=jax.ShapeDtypeStruct(x.shape, x.dtype),
-        input_output_aliases={0: 0},
-        cost_estimate=SMALL,
-        name="tie",
-    )(x, after)
+def entire(x):
+    return pl.BlockSpec(x.shape, lambda i: (0, 0))
 
 
 def summed(x):
@@ -166,8 +143,19 @@
     return high, (x - high.astype(F32)).astype(BF16)
 
 
-def blended_kernel(side_ref, cross_ref, latent_ref, momentum_gram_ref, squares_ref, kept_ref, sent_ref, note_ref, gram_ref):
+def blended_kernel(side_ref, origin_ref, cross_ref, momentum_gram_ref, squares_ref, *refs):
+    held_refs, (latent_ref, kept_ref, sent_ref, note_ref, gram_ref) = refs[:-5], refs[-5:]
     tasks, size = latent_ref.shape
+    held = jnp.concatenate([ref[...] for ref in held_refs], axis=0)
+    origin = jnp.broadcast_to(origin_ref[...], (tasks, tasks))
+    lane = lax.broadcasted_iota(jnp.int32, (tasks, LANES), 1)
+    digits = held[:, size:].astype(F32) * jnp.where(lane == 0, 256.0, jnp.where(lane == 1, 1.0, 0.0))
+    row = lax.broadcasted_iota(jnp.int32, (tasks, tasks), 1).astype(F32)
+    ids = jnp.where(origin == row, jnp.sum(digits, axis=1, keepdims=True), 0.0)
+    chosen = (origin == jnp.sum(ids, axis=0, keepdims=True)).astype(F32).astype(BF16)
+    latent_ref[...] = lax.dot_general(
+        chosen, held[:, :size], (((0,), (0,)), ((), ())), preferred_element_type=F32
+    ).astype(BF16)
     alpha, beta = MOMENTUM_DECAY**2, 1.0 + MOMENTUM_DECAY
     latent = latent_ref[...]
     turned = latent.astype(F32).T.astype(BF16)
@@ -197,25 +185,27 @@
     note_ref[...] = note.astype(BF16)
 
 
-def blended_gram(side, cross, latent, gram, squares):
+def blended_gram(side, origin, cross, gram, squares, held):
     half = gram.shape[0] // 2
-    whole = pl.BlockSpec(memory_space=pltpu.VMEM)
+    tasks, size = origin.shape[0], held[0].shape[1] - LANES
+    operands = (origin, cross, gram, squares, *held)
+    results = [
+        jax.ShapeDtypeStruct((tasks, size), BF16),
+        jax.ShapeDtypeStruct((half, BLOCK), F32),
+        jax.ShapeDtypeStruct((half, BLOCK), BF16),
+        jax.ShapeDtypeStruct((16, BLOCK), BF16),
+    ]
     return pl.pallas_call(
         blended_kernel,
-        in_specs=[pl.BlockSpec(memory_space=pltpu.SMEM), whole, whole, whole, whole],
-        out_specs=[whole, whole, whole],
-        out_shape=[
-            jax.ShapeDtypeStruct((half, BLOCK), F32),
-            jax.ShapeDtypeStruct((half, BLOCK), BF16),
-            jax.ShapeDtypeStruct((16, BLOCK), BF16),
-        ],
+        grid=(1,),
+        in_specs=[pl.BlockSpec(memory_space=pltpu.SMEM)] + [entire(x) for x in operands],
+        out_specs=[entire(x) for x in results],
+        out_shape=results,
         scratch_shapes=[pltpu.VMEM(gram.shape, F32)],
-        compiler_params=pltpu.CompilerParams(vmem_limit_bytes=40 * 2**20),
-        cost_estimate=pl.CostEstimate(
-            flops=4 * latent.shape[0] * latent.shape[1] ** 2, bytes_accessed=8 * gram.size, transcendentals=0
-        ),
+        compiler_params=pltpu.CompilerParams(vmem_limit_bytes=63 * 2**20),
+        cost_estimate=pl.CostEstimate(flops=4 * tasks * size**2, bytes_accessed=8 * gram.size, transcendentals=0),
         name="blended_gram",
-    )(side, cross, latent, gram, squares)
+    )(side, *operands)
 
 
 def momentum_kernel(latent_ref, momentum_ref, columns_ref, *refs):
@@ -246,11 +236,11 @@
         + [anywhere] * (len(operands) - 3),
         out_specs=[
             pl.BlockSpec((size, tile), lambda i: (0, i + first)),
-            pl.BlockSpec((8, LANES), lambda i: (0, 0)),
+            pl.BlockSpec((1, BLOCK), lambda i: (0, 0)),
         ],
         out_shape=[
             jax.ShapeDtypeStruct((size, count), F32),
-            jax.ShapeDtypeStruct((8, LANES), F32),
+            jax.ShapeDtypeStruct((1, BLOCK), F32),
         ],
         input_output_aliases={} if held is None else {4: 0},
         compiler_params=pltpu.CompilerParams(vmem_limit_bytes=56 * 2**20),
@@ -259,7 +249,7 @@
     )(*operands)
 
 
-def poly_kernel(notes_ref, gram_ref, latent_ref, weight_ref, inverse_ref, x_ref, xb_ref, p_ref, pb_ref, d_ref):
+def poly_kernel(notes_ref, scale_ref, gram_ref, latent_ref, weight_ref, factor_ref, x_ref, xb_ref, p_ref, pb_ref, d_ref, g_ref):
     size = x_ref.shape[0]
     tasks = latent_ref.shape[0]
     blocks = size // BLOCK
@@ -271,78 +261,87 @@
 
     turned = latent_ref[...].astype(F32).T.astype(BF16)
     norm = jnp.sqrt(jnp.maximum(summed(notes_ref[...].astype(F32)), 0.0)) + EPSILON
-    inverse_ref[...] = jnp.broadcast_to(1.0 / norm, inverse_ref.shape)
+    whole = a * a * MOMENTUM_DECAY**2
+    factor_ref[...] = scale_ref[...] * (whole / norm)
     inverse = 1.0 / (norm * norm)
+
+    def product(left_ref, right_ref, j):
+        return dot(left_ref[: (j + 1) * BLOCK, :], right_ref[:, part(j)])
+
+    def spread(ref, j, value):
+        ref[: (j + 1) * BLOCK, part(j)] = value.astype(BF16)
+        for i in range(j):
+            ref[part(j), part(i)] = value[part(i), :].T.astype(BF16)
 
     for at, (i, j) in enumerate(upper_blocks(blocks)):
         block = gram_ref[part(at), :].astype(F32) * inverse
         x_ref[part(i), part(j)] = block
         xb_ref[part(i), part(j)] = block.astype(BF16)
         if i != j:
-            x_ref[part(j), part(i)] = block.T
             xb_ref[part(j), part(i)] = block.T.astype(BF16)
-    for j in range(blocks):
-        poly = b * x_ref[:, part(j)] + c * dot(xb_ref[...], xb_ref[:, part(j)])
-        p_ref[:, part(j)] = poly
-        pb_ref[:, part(j)] = poly.astype(BF16)
-    for j in range(blocks):
-        d_ref[:, part(j)] = (
-            2 * a * p_ref[:, part(j)] + dot(pb_ref[...], pb_ref[:, part(j)])
-        ).astype(BF16)
-    for j in range(blocks):
-        x_ref[:, part(j)] = a * a * x_ref[:, part(j)] + dot(xb_ref[...], d_ref[:, part(j)])
-    xb_ref[...] = x_ref[...].astype(BF16)
-    for j in range(blocks):
-        poly = b * x_ref[:, part(j)] + c * dot(xb_ref[...], xb_ref[:, part(j)])
-        p_ref[:, part(j)] = p_ref[:, part(j)] + poly
-        d_ref[:, part(j)] = poly.astype(BF16)
-    for j in range(blocks):
-        rest = a * p_ref[:, part(j)] + dot(d_ref[...], pb_ref[:, part(j)])
-        xb_ref[:, part(j)] = rest.astype(BF16)
-        weight_ref[:, part(j)] = (MOMENTUM_DECAY**2 * rest).astype(BF16)
-    side = beta * (a * a * turned.astype(F32) + dot(xb_ref[...], turned))
+    upper = [(j, slice(0, (j + 1) * BLOCK)) for j in range(blocks)]
+    for j, rows in upper:
+        poly = b * x_ref[rows, part(j)] + c * product(xb_ref, xb_ref, j)
+        p_ref[rows, part(j)] = poly
+        spread(pb_ref, j, poly)
+    for j, rows in upper:
+        spread(d_ref, j, 2 * a * p_ref[rows, part(j)] + product(pb_ref, pb_ref, j))
+    for j, rows in upper:
+        gram = a * a * x_ref[rows, part(j)] + product(xb_ref, d_ref, j)
+        x_ref[rows, part(j)] = gram
+        spread(g_ref, j, gram)
+    for j, rows in upper:
+        poly = b * x_ref[rows, part(j)] + c * product(g_ref, g_ref, j)
+        p_ref[rows, part(j)] = p_ref[rows, part(j)] + poly
+        spread(d_ref, j, poly)
+    for j, rows in upper:
+        rest = a * p_ref[rows, part(j)] + product(d_ref, pb_ref, j)
+        spread(xb_ref, j, rest)
+        spread(weight_ref, j, (MOMENTUM_DECAY**2 / whole) * rest)
+    side = (beta / whole) * (a * a * turned.astype(F32) + dot(xb_ref[...], turned))
     high = side.astype(BF16)
     weight_ref[:, size : size + tasks] = high
     weight_ref[:, size + tasks :] = (side - high.astype(F32)).astype(BF16)
 
 
-def poly_pass(notes, gram, latent):
+def poly_pass(notes, scale, gram, latent):
     tasks, size = latent.shape
-    whole = pl.BlockSpec(memory_space=pltpu.VMEM)
+    operands = (notes, scale, gram, latent)
+    results = [
+        jax.ShapeDtypeStruct((size, size + 2 * tasks), BF16),
+        jax.ShapeDtypeStruct(scale.shape, F32),
+    ]
     return pl.pallas_call(
         poly_kernel,
-        in_specs=[whole, whole, whole],
-        out_specs=[whole, whole],
-        out_shape=[
-            jax.ShapeDtypeStruct((size, size + 2 * tasks), BF16),
-            jax.ShapeDtypeStruct((8, LANES), F32),
-        ],
+        grid=(1,),
+        in_specs=[entire(x) for x in operands],
+        out_specs=[entire(x) for x in results],
+        out_shape=results,
         scratch_shapes=[
             pltpu.VMEM((size, size), F32),
             pltpu.VMEM((size, size), BF16),
             pltpu.VMEM((size, size), F32),
             pltpu.VMEM((size, size), BF16),
             pltpu.VMEM((size, size), BF16),
+            pltpu.VMEM((size, size), BF16),
         ],
         compiler_params=pltpu.CompilerParams(vmem_limit_bytes=50 * 2**20),
         cost_estimate=pl.CostEstimate(flops=10 * size**3, bytes_accessed=4 * size * size, transcendentals=0),
         name="polynomial",
-    )(notes, gram, latent)
-
-
-def step_kernel(weight_ref, inverse_ref, scale_ref, momentum_ref, columns_ref, step_ref, right_ref):
+    )(*operands)
+
+
+def step_kernel(weight_ref, factor_ref, momentum_ref, columns_ref, step_ref, right_ref):
     momentum = momentum_ref[...]
     size = momentum.shape[0]
     tasks = columns_ref.shape[0]
     right_ref[:size, :] = momentum.astype(BF16)
     right_ref[size : size + tasks, :] = columns_ref[...]
     right_ref[size + tasks :, :] = columns_ref[...]
-    factor = NEWTON_A**2 * MOMENTUM_DECAY**2
-    scale = scale_ref[...] * inverse_ref[0:1, 0:1]
-    step_ref[...] = scale * (factor * momentum + dot(weight_ref[...], right_ref[...]))
-
-
-def step_pass(weight, inverse, scale, momentum, columns):
+    step_ref[...] = factor_ref[...] * (momentum + dot(weight_ref[...], right_ref[...]))
+
+
+def step_pass(weight, factor, momentum, columns):
     size, count = momentum.shape
     tasks = columns.shape[0]
     depth = weight.shape[1]
@@ -352,7 +351,6 @@
         grid=(count // tile,),
         in_specs=[
             pl.BlockSpec((size, depth), lambda i: (0, 0)),
-            pl.BlockSpec((8, LANES), lambda i: (0, 0)),
             pl.BlockSpec((1, tile), lambda i: (0, i)),
             pl.BlockSpec((size, tile), lambda i: (0, i)),
             pl.BlockSpec((tasks, tile), lambda i: (0, i)),
@@ -365,7 +363,7 @@
             flops=2 * count * size * depth, bytes_accessed=8 * size * count, transcendentals=0
         ),
         name="step",
-    )(weight, inverse, scale, momentum, columns)
+    )(weight, factor, momentum, columns)
 
 
 def halves(gram, distance, me):
@@ -393,16 +391,14 @@
     held = with_ids(latents, task_ids)
     rounded, gram, squares = gram_pass(momentum)
     cross = cross_pass(columns, rounded)
-    for place, distance in enumerate(distances):
-        got = swap(held, distance, count)
-        if place == len(distances) - 2:
-            got = tied(got, squares)
-        if place == len(distances) - 1:
-            got = tied(got, cross)
-        held = jnp.concatenate([held, got], axis=0)
-    latent = chosen_latents(held, me, rows, size)
-    side = me % 2
-    kept, sent, note = blended_gram(side.astype(jnp.int32).reshape(1), cross, latent, gram, squares)
+    for distance in distances[:-2]:
+        held = jnp.concatenate([held, swap(held, distance, count)], axis=0)
+    quarter = count // 4
+    far = [swap(held, k * quarter, count) for k in (1, 2, 3)]
+    place = jnp.arange(rows * count, dtype=jnp.int32)
+    origin = (((place // rows) ^ me) * rows + place % rows).astype(F32).reshape(-1, 1)
+    side = (me % 2).astype(jnp.int32).reshape(1)
+    latent, kept, sent, note = blended_gram(side, origin, cross, gram, squares, [held] + far)
 
     new_momentum = None
     for place, distance in enumerate(distances):
@@ -413,7 +409,7 @@
             new_momentum, mark = momentum_piece(
                 latent, momentum, columns, sent, new_momentum, place - PIECES_AT[0], PIECES
             )
-            got = tied(got, mark)
+            kept = kept + mark
         gram = kept + got.astype(F32)
     shard = gram.shape[0]
     gram = jnp.concatenate([gram.astype(BF16), note], axis=0)
@@ -423,7 +419,7 @@
             new_momentum, mark = momentum_piece(
                 latent, momentum, columns, gram, new_momentum, PIECES - 1, PIECES
             )
-            got = tied(got, mark)
+            got = got + mark.astype(BF16)
         if distance > 1:
             gram = doubled(gram, got, distance, me)
     apart = [x.reshape(count // 2, -1, BLOCK) for x in (gram, got)]
@@ -431,14 +427,13 @@
     gram, got = [x[:, :shard].reshape(-1, BLOCK) for x in apart]
     gram = doubled(gram, got, 1, me)
 
-    weight, inverse = poly_pass(notes, gram, latent)
-
     column = me * column_count + jnp.arange(column_count, dtype=jnp.int32)
     after = jnp.concatenate([offsets[1:], jnp.full((1,), out_total, offsets.dtype)])
     inside = (column[None, :] >= offsets[:, None]) & (column[None, :] < after[:, None])
     column_scale = jnp.sum(jnp.where(inside, target_scale[:, None], 0.0), axis=0, keepdims=True)
     scale = column_scale * math.sqrt(out_total)
-    step = step_pass(weight, inverse, scale, momentum, columns)
+    weight, factor = poly_pass(notes, scale, gram, latent)
+    step = step_pass(weight, factor, momentum, columns)
     return new_momentum, step
 
 

time: 168 us -> 162 us (0.964)
  local copies, waits for them, and re-layouts: 11.9 us -> 3.16 us
  waiting for transfers between devices: 28.8 us -> 37.4 us
  starting transfers between devices: 32.1 us -> 26.3 us
    ppermute x15 -> x16, starting transfers between devices: 24.8 us -> 19 us  [swap(): return lax.ppermute(x, AXES, [(i, i ^ distance) for i in range(count)])]
    all_to_all x1, waiting for transfers between devices: 0.01 us -> 4.81 us  [per_device(): lax.all_to_all(factor_grads, AXES, split_axis=1, concat_axis=0, tiled=True)]
    concatenate x2 -> x0, local copies, waits for them, and re-layouts: 4.41 us -> none  [per_device(): held = jnp.concatenate([held, got], axis=0)]
    unnamed x54 -> x28, local copies, waits for them, and re-layouts: 5.75 us -> 1.41 us
    ppermute x15 -> x16, waiting for transfers between devices: 28.8 us -> 32.6 us  [swap(): return lax.ppermute(x, AXES, [(i, i ^ distance) for i in range(count)])]
    pallas_call x7 -> x2, Pallas kernels: 15.1 us -> 15.9 us  [the longest x1 11 us: poly_pass(): pl.pallas_call(poly_kernel, grid=(1,), in_specs=[entire(x) for x in opera...]
  transfers between devices with their start and end apart: 16 -> 17, of which waited for: 11 -> 11; matrix products, arithmetic and copies ran while one was open for 3% -> 2% of each run, Pallas kernels for 28% -> 29%
where the time goes in v2:
time: 162 us; the launch traced here: 161 us
  Pallas kernels  87.3 us (54%)
  waiting for transfers between devices  37.4 us (23%)
  starting transfers between devices  26.3 us (16%)
  other arithmetic  5.81 us (4%)
  local copies, waits for them, and re-layouts  3.16 us (2%)
    ppermute x16, waiting for transfers between devices, swap(): return lax.ppermute(x, AXES, [(i, i ^ distance) for i in range(count)])  32.6 us
    pallas_call x1, Pallas kernels, step_pass(): pl.pallas_call(step_kernel, grid=(count // tile,), in_specs=[pl.BlockSpec...  24.4 us
    pallas_call x3, Pallas kernels, momentum_piece(): pl.pallas_call(momentum_kernel, grid=(steps,), in_specs=[pl.BlockSpec((ta...  19.4 us
    ppermute x16, starting transfers between devices, swap(): return lax.ppermute(x, AXES, [(i, i ^ distance) for i in range(count)])  19 us
    pallas_call x1, Pallas kernels, gram_pass(): pl.pallas_call(gram_kernel, grid=(count // tile,), in_specs=[pl.BlockSpec...  18.8 us
    pallas_call x1, Pallas kernels, poly_pass(): pl.pallas_call(poly_kernel, grid=(1,), in_specs=[entire(x) for x in opera...  11 us
    pallas_call x1, Pallas kernels, cross_pass(): pl.pallas_call(cross_kernel, grid=(count // tile,), in_specs=[pl.BlockSpe...  8.88 us
    all_to_all x1, starting transfers between devices, per_device(): lax.all_to_all(factor_grads, AXES, split_axis=1, concat_axis=0, tiled=True)  7.3 us
  transfers between devices with their start and end apart: 17, of which 11 were waited for; matrix products, arithmetic and copies ran while one was open for 2% of the time, Pallas kernels for 29%

profile of v2, /device:TPU:0, one launch (start us, length us, event | category | flops | bytes accessed | tf_op | source)
XLA Modules:
  0.0 161.1 jit_solution(10309811665531865343)
XLA Ops:
  0.6 7.3 %all-to-all-start = ((bf16[4,32,6144]{2,0,1:T(4,128)(2,1)}), bf16[4,32,6144]{2,0,1:T(4,128)(2,1)S(1)}, u32[]{:S(2)}, u32[]{:S(2)}) async-start(bf16[4,32,6144]{2,0,1:T(4,128)(2,1)} %bitcast.24), calls=%async_computation | async-start | bytes 3145728 | tf_op jit(solution)/shard_map/all_to_all | solution.py:390
  8.0 0.1 copy.27
  8.1 0.1 copy.28
  8.2 0.1 fusion.13
  8.3 0.3 collective-permute-start
  8.6 0.9 collective-permute-done
  9.6 1.8 %collective-permute-start.1 = (bf16[8,1152]{1,0:T(8,128)(2,1)S(1)}, bf16[8,1152]{1,0:T(8,128)(2,1)S(1)}, u32[]{:S(2)}, u32[]{:S(2)}) collective-permute-start(bf16[8,1152]{1,0:T(8,128)(2,1)S(1)} %pad_maximum_fusion.8), channel_id=1, source_target_pairs={{0,2},{1,3},{2,0},{3,1},{4,6},{5,7},{6,4},{7,5},{8,10},{9,11},{10,... | collective-permute-start | bytes 55304 | tf_op jit(solution)/shard_map/ppermute | solution.py:36
  11.4 2.6 %collective-permute-done.1 = bf16[8,1152]{1,0:T(8,128)(2,1)S(1)} collective-permute-done((bf16[8,1152]{1,0:T(8,128)(2,1)S(1)}, bf16[8,1152]{1,0:T(8,128)(2,1)S(1)}, u32[]{:S(2)}, u32[]{:S(2)}) %collective-permute-start.1) | collective-permute-done | bytes 18464 | tf_op jit(solution)/shard_map/ppermute | solution.py:36
  14.0 6.3 %collective-permute-start.2 = (bf16[16,1152]{1,0:T(8,128)(2,1)S(1)}, bf16[16,1152]{1,0:T(8,128)(2,1)S(1)}, u32[]{:S(2)}, u32[]{:S(2)}) collective-permute-start(bf16[16,1152]{1,0:T(8,128)(2,1)S(1)} %pad_maximum_fusion.7), channel_id=1, source_target_pairs={{0,4},{1,5},{2,6},{3,7},{4,0},{5,1},{6,2},{7,3},{8,12},{9,13},{10,... | collective-permute-start | bytes 110600 | tf_op jit(solution)/shard_map/ppermute | solution.py:36
  20.3 0.6 fusion.9.origin_ref
  21.0 18.8 %momentum_gram.1 = (bf16[1024,6144]{1,0:T(8,128)(2,1)}, f32[2560,256]{1,0:T(8,128)}, f32[8,128]{1,0:T(8,128)}) custom-call(f32[1024,6144]{1,0:T(8,128)} %momentum_ref.9), custom_call_target="tpu_custom_call" | custom-call | flops 1 | bytes 1 | tf_op jit(solution)/shard_map/momentum_gram/pallas_call | solution.py:87
  39.8 0.0 collective-permute-done.2
  39.8 1.5 collective-permute-start.5
  41.3 0.8 collective-permute-start.4
  42.1 2.2 %collective-permute-start.3 = (bf16[32,1152]{1,0:T(8,128)(2,1)S(1)}, bf16[32,1152]{1,0:T(8,128)(2,1)S(1)}, u32[]{:S(2)}, u32[]{:S(2)}) collective-permute-start(bf16[32,1152]{1,0:T(8,128)(2,1)S(1)} %pad_maximum_fusion.5.refs_0_), channel_id=1, source_target_pairs={{0,8},{1,9},{2,10},{3,11},{4,12},{5,13},{6,14},{7,15},{8,0},{9,1},... | collective-permute-start | bytes 221192 | tf_op jit(solution)/shard_map/ppermute | solution.py:36
  44.3 4.8 %all-to-all-done = bf16[4,32,6144]{2,0,1:T(4,128)(2,1)S(1)} async-done(((bf16[4,32,6144]{2,0,1:T(4,128)(2,1)}), bf16[4,32,6144]{2,0,1:T(4,128)(2,1)S(1)}, u32[]{:S(2)}, u32[]{:S(2)}) %all-to-all-start) | async-done | bytes 1572896 | tf_op jit(solution)/shard_map/all_to_all | solution.py:390
  49.1 1.3 all_to_all.17.columns_ref
  50.4 8.9 %cross_terms.1.cross_ref = f32[128,1152]{1,0:T(8,128)} custom-call(bf16[128,6144]{1,0:T(8,128)(2,1)} %all_to_all.17.columns_ref, bf16[1024,6144]{1,0:T(8,128)(2,1)} %get-tuple-element.17.rounded_ref), custom_call_target="tpu_custom_call" | custom-call | flops 1610612736 | bytes 12582912 | tf_op jit(solution)/shard_map/cross_terms/pallas_call | solution.py:124
  59.3 0.0 collective-permute-done.5.refs_3_
  59.3 0.0 collective-permute-done.3.refs_1_
  59.4 0.6 copy-done.7
  59.9 0.0 copy-done.8
  60.0 0.0 copy-done.9
  60.0 4.8 %blended_gram.1 = (bf16[128,1024]{1,0:T(8,128)(2,1)}, f32[1280,256]{1,0:T(8,128)}, bf16[1280,256]{1,0:T(8,128)(2,1)}, bf16[16,256]{1,0:T(8,128)(2,1)}) custom-call(s32[1]{0:T(128)} %bitcast.side_ref, f32[128,1]{1,0:T(8,128)} %fusion.9.origin_ref, f32[128,1152]{1,0:T(8,128)} %cross_terms.1.cross_ref, f32[2560,256]{1,0:T(8,128)} %get-tuple-element.18.momentum_gram_ref, ...), custom_call_target="tpu_custom_call" | custom-call | flops 536870912 | bytes 5242880 | tf_op jit(solution)/shard_map/blended_gram/pallas_call | solution.py:198
  64.9 0.0 collective-permute-start.6
  64.9 2.3 %collective-permute-done.6 = bf16[1280,256]{1,0:T(8,128)(2,1)S(1)} collective-permute-done((bf16[1280,256]{1,0:T(8,128)(2,1)}, bf16[1280,256]{1,0:T(8,128)(2,1)S(1)}, u32[]{:S(2)}, u32[]{:S(2)}) %collective-permute-start.6) | collective-permute-done | bytes 655392 | tf_op jit(solution)/shard_map/ppermute | solution.py:36
  67.2 1.4 convert_add_fusion
  68.7 0.0 copy-start.3
  68.7 1.5 collective-permute-start.7
  70.2 6.5 %new_momentum.3 = (f32[1024,6144]{1,0:T(8,128)}, f32[1,256]{1,0:T(1,128)}) custom-call(bf16[128,1024]{1,0:T(8,128)(2,1)} %get-tuple-element.20.latent_ref, f32[1024,6144]{1,0:T(8,128)} %momentum_ref.9, bf16[128,6144]{1,0:T(8,128)(2,1)} %all_to_all.17.columns_ref, bf16[640,256]{1,0:T(8,128)(2,1)} %copy-done.3), custom_call_target="tpu_custom_call" | custom-call | flops 1 | bytes 1 | tf_op jit(solution)/shard_map/new_momentum/pallas_call | solution.py:228
  76.7 1.8 %collective-permute-done.7 = bf16[640,256]{1,0:T(8,128)(2,1)S(1)} collective-permute-done((bf16[640,256]{1,0:T(8,128)(2,1)S(1)}, bf16[640,256]{1,0:T(8,128)(2,1)S(1)}, u32[]{:S(2)}, u32[]{:S(2)}) %collective-permute-start.7) | collective-permute-done | bytes 327712 | tf_op jit(solution)/shard_map/ppermute | solution.py:36
  78.5 0.7 convert_add_fusion.1
  79.3 0.0 copy-start.4
  79.3 1.5 collective-permute-start.8
  80.8 6.4 %new_momentum.4 = (f32[1024,6144]{1,0:T(8,128)}, f32[1,256]{1,0:T(1,128)}) custom-call(bf16[128,1024]{1,0:T(8,128)(2,1)} %get-tuple-element.20.latent_ref, f32[1024,6144]{1,0:T(8,128)} %momentum_ref.9, bf16[128,6144]{1,0:T(8,128)(2,1)} %all_to_all.17.columns_ref, bf16[320,256]{1,0:T(8,128)(2,1)} %copy-done.4, ...), custom_call_target="tpu_custom_call", output_to_operand_aliasing={{0}: (4, {})} | custom-call | flops 1 | bytes 1 | tf_op jit(solution)/shard_map/new_momentum/pallas_call | solution.py:228
  87.2 0.7 convert_add_fusion.2
  87.9 0.1 collective-permute-start.9
  88.1 4.4 %collective-permute-done.9 = bf16[160,256]{1,0:T(8,128)(2,1)S(1)} collective-permute-done((bf16[160,256]{1,0:T(8,128)(2,1)S(1)}, bf16[160,256]{1,0:T(8,128)(2,1)S(1)}, u32[]{:S(2)}, u32[]{:S(2)}) %collective-permute-start.9) | collective-permute-done | bytes 81952 | tf_op jit(solution)/shard_map/ppermute | solution.py:36
  92.5 0.1 collective-permute-start.10
  92.6 4.9 %collective-permute-done.10 = bf16[80,256]{1,0:T(8,128)(2,1)S(1)} collective-permute-done((bf16[80,256]{1,0:T(8,128)(2,1)S(1)}, bf16[80,256]{1,0:T(8,128)(2,1)S(1)}, u32[]{:S(2)}, u32[]{:S(2)}) %collective-permute-start.10) | collective-permute-done | bytes 40992 | tf_op jit(solution)/shard_map/ppermute | solution.py:36
  97.5 0.1 collective-permute-start.11
  97.6 5.2 %collective-permute-done.11 = bf16[96,256]{1,0:T(8,128)(2,1)S(1)} collective-permute-done((bf16[96,256]{1,0:T(8,128)(2,1)S(1)}, bf16[96,256]{1,0:T(8,128)(2,1)S(1)}, u32[]{:S(2)}, u32[]{:S(2)}) %collective-permute-start.11) | collective-permute-done | bytes 49184 | tf_op jit(solution)/shard_map/ppermute | solution.py:36
  102.8 0.3 collective-permute-start.12
  103.1 4.4 %collective-permute-done.12 = bf16[192,256]{1,0:T(8,128)(2,1)S(1)} collective-permute-done((bf16[192,256]{1,0:T(8,128)(2,1)S(1)}, bf16[192,256]{1,0:T(8,128)(2,1)S(1)}, u32[]{:S(2)}, u32[]{:S(2)}) %collective-permute-start.12) | collective-permute-done | bytes 98336 | tf_op jit(solution)/shard_map/ppermute | solution.py:36
  107.5 0.8 collective-permute-start.13
  108.4 4.9 %collective-permute-done.13 = bf16[384,256]{1,0:T(8,128)(2,1)S(1)} collective-permute-done((bf16[384,256]{1,0:T(8,128)(2,1)S(1)}, bf16[384,256]{1,0:T(8,128)(2,1)S(1)}, u32[]{:S(2)}, u32[]{:S(2)}) %collective-permute-start.13) | collective-permute-done | bytes 196640 | tf_op jit(solution)/shard_map/ppermute | solution.py:36
  113.3 0.1 broadcast_select_fusion.5
  113.4 0.0 copy-start.2
  113.4 1.6 collective-permute-start.14
  115.0 6.4 %new_momentum.5 = (f32[1024,6144]{1,0:T(8,128)}, f32[1,256]{1,0:T(1,128)}) custom-call(bf16[128,1024]{1,0:T(8,128)(2,1)} %get-tuple-element.20.latent_ref, f32[1024,6144]{1,0:T(8,128)} %momentum_ref.9, bf16[128,6144]{1,0:T(8,128)(2,1)} %all_to_all.17.columns_ref, bf16[768,256]{1,0:T(8,128)(2,1)} %copy-done.2, ...), custom_call_target="tpu_custom_call", output_to_operand_aliasing={{0}: (4, {})} | custom-call | flops 1 | bytes 1 | tf_op jit(solution)/shard_map/new_momentum/pallas_call | solution.py:228
  121.4 0.7 convert_reduce_fusion
  122.1 0.0 collective-permute-done.14
  122.1 0.2 broadcast_select_fusion.3
  122.3 0.1 pad_maximum_fusion.1
  122.4 0.1 collective-permute-start.15
  122.5 0.1 slice.17
  122.5 0.1 pad_add_fusion
  122.6 0.8 select_reduce_fusion
  123.4 1.3 collective-permute-done.15
  124.7 0.1 broadcast_select_fusion.1
  124.9 0.1 pad_maximum_fusion.gram_ref
  125.0 0.7 copy-done.1
  125.7 11.0 %polynomial.1 = (bf16[1024,1280]{1,0:T(8,128)(2,1)}, f32[1,6144]{1,0:T(1,128)S(1)}) custom-call(bf16[32,256]{1,0:T(8,128)(2,1)S(1)} %pad_maximum_fusion.9.notes_ref, f32[1,6144]{1,0:T(1,128)S(1)} %bitcast.18, bf16[2560,256]{1,0:T(8,128)(2,1)S(1)} %pad_maximum_fusion.gram_ref, bf16[128,1024]{1,0:T(8,128)(2,1)S(1)} %copy-done.1), custom_call_target="tpu_custom_call" | custom-call | flops 10737418240 | bytes 4194304 | tf_op jit(solution)/shard_map/polynomial/pallas_call | solution.py:314
  136.7 24.4 %step.1 = f32[1024,6144]{1,0:T(8,128)} custom-call(bf16[1024,1280]{1,0:T(8,128)(2,1)} %get-tuple-element.30.weight_ref, f32[1,6144]{1,0:T(1,128)S(1)} %get-tuple-element.31.factor_ref, f32[1024,6144]{1,0:T(8,128)} %momentum_ref.9, bf16[128,6144]{1,0:T(8,128)(2,1)S(1)} %copy-done), custom_call_target="tpu_custom_call" | custom-call | flops 16106127360 | bytes 50331648 | tf_op jit(solution)/shard_map/step/pallas_call | solution.py:349
  (46 shorter events, 0.4 us)
Async XLA Ops:
  0.6 7.3 %copy-start.13 = (s32[4]{0:T(128)S(1)}, s32[4]{0:T(128)}, u32[]{:S(2)}) copy-start(s32[4]{0:T(128)} %param.8) | copy-start | bytes 52
  0.6 7.6 %copy-start.6 = (bf16[4,1024]{1,0:T(4,128)(2,1)S(1)}, bf16[4,1024]{1,0:T(4,128)(2,1)}, u32[]{:S(2)}) copy-start(bf16[4,1024]{1,0:T(4,128)(2,1)} %param.7) | copy-start | bytes 24580
  0.6 48.5 %all-to-all-start = ((bf16[4,32,6144]{2,0,1:T(4,128)(2,1)}), bf16[4,32,6144]{2,0,1:T(4,128)(2,1)S(1)}, u32[]{:S(2)}, u32[]{:S(2)}) async-start(bf16[4,32,6144]{2,0,1:T(4,128)(2,1)} %bitcast.24), calls=%async_computation | async-start | bytes 3145728 | tf_op jit(solution)/shard_map/all_to_all | solution.py:390
  8.3 1.2 collective-permute-start
  9.6 4.4 %collective-permute-start.1 = (bf16[8,1152]{1,0:T(8,128)(2,1)S(1)}, bf16[8,1152]{1,0:T(8,128)(2,1)S(1)}, u32[]{:S(2)}, u32[]{:S(2)}) collective-permute-start(bf16[8,1152]{1,0:T(8,128)(2,1)S(1)} %pad_maximum_fusion.8), channel_id=1, source_target_pairs={{0,2},{1,3},{2,0},{3,1},{4,6},{5,7},{6,4},{7,5},{8,10},{9,11},{10,... | collective-permute-start | bytes 55304 | tf_op jit(solution)/shard_map/ppermute | solution.py:36
  14.0 25.8 %collective-permute-start.2 = (bf16[16,1152]{1,0:T(8,128)(2,1)S(1)}, bf16[16,1152]{1,0:T(8,128)(2,1)S(1)}, u32[]{:S(2)}, u32[]{:S(2)}) collective-permute-start(bf16[16,1152]{1,0:T(8,128)(2,1)S(1)} %pad_maximum_fusion.7), channel_id=1, source_target_pairs={{0,4},{1,5},{2,6},{3,7},{4,0},{5,1},{6,2},{7,3},{8,12},{9,13},{10,... | collective-permute-start | bytes 110600 | tf_op jit(solution)/shard_map/ppermute | solution.py:36
  39.8 19.5 %copy-start.5 = (bf16[32,1152]{1,0:T(8,128)(2,1)}, bf16[32,1152]{1,0:T(8,128)(2,1)S(1)}, u32[]{:S(2)}) copy-start(bf16[32,1152]{1,0:T(8,128)(2,1)S(1)} %pad_maximum_fusion.5.refs_0_) | copy-start | bytes 221188
  39.8 19.5 %collective-permute-start.5 = (bf16[32,1152]{1,0:T(8,128)(2,1)S(1)}, bf16[32,1152]{1,0:T(8,128)(2,1)S(1)}, u32[]{:S(2)}, u32[]{:S(2)}) collective-permute-start(bf16[32,1152]{1,0:T(8,128)(2,1)S(1)} %pad_maximum_fusion.5.refs_0_), channel_id=1, source_target_pairs={{0,24},{1,25},{2,26},{3,27},{4,28},{5,29},{6,30},{7,31},{8,16},{9,... | collective-permute-start | bytes 221192 | tf_op jit(solution)/shard_map/ppermute | solution.py:36
  41.3 18.0 %collective-permute-start.4 = (bf16[32,1152]{1,0:T(8,128)(2,1)S(1)}, bf16[32,1152]{1,0:T(8,128)(2,1)S(1)}, u32[]{:S(2)}, u32[]{:S(2)}) collective-permute-start(bf16[32,1152]{1,0:T(8,128)(2,1)S(1)} %pad_maximum_fusion.5.refs_0_), channel_id=1, source_target_pairs={{0,16},{1,17},{2,18},{3,19},{4,20},{5,21},{6,22},{7,23},{8,24},{9,... | collective-permute-start | bytes 221192 | tf_op jit(solution)/shard_map/ppermute | solution.py:36
  42.1 17.3 %collective-permute-start.3 = (bf16[32,1152]{1,0:T(8,128)(2,1)S(1)}, bf16[32,1152]{1,0:T(8,128)(2,1)S(1)}, u32[]{:S(2)}, u32[]{:S(2)}) collective-permute-start(bf16[32,1152]{1,0:T(8,128)(2,1)S(1)} %pad_maximum_fusion.5.refs_0_), channel_id=1, source_target_pairs={{0,8},{1,9},{2,10},{3,11},{4,12},{5,13},{6,14},{7,15},{8,0},{9,1},... | collective-permute-start | bytes 221192 | tf_op jit(solution)/shard_map/ppermute | solution.py:36
  59.3 0.6 copy-start.7
  59.3 0.7 copy-start.8
  59.4 0.6 copy-start.9
  64.9 2.3 %collective-permute-start.6 = (bf16[1280,256]{1,0:T(8,128)(2,1)}, bf16[1280,256]{1,0:T(8,128)(2,1)S(1)}, u32[]{:S(2)}, u32[]{:S(2)}) collective-permute-start(bf16[1280,256]{1,0:T(8,128)(2,1)} %get-tuple-element.22), channel_id=1, source_target_pairs={{0,1},{1,0},{2,3},{3,2},{4,5},{5,4},{6,7},{7,6},{8,9},{9,8},{10,11... | collective-permute-start | bytes 1966088 | tf_op jit(solution)/shard_map/ppermute | solution.py:36
  68.7 1.5 copy-start.3
  68.7 9.8 %collective-permute-start.7 = (bf16[640,256]{1,0:T(8,128)(2,1)S(1)}, bf16[640,256]{1,0:T(8,128)(2,1)S(1)}, u32[]{:S(2)}, u32[]{:S(2)}) collective-permute-start(bf16[640,256]{1,0:T(8,128)(2,1)S(1)} %dynamic-slice_convert_fusion.refs_0_), channel_id=1, source_target_pairs={{0,2},{1,3},{2,0},{3,1},{4,6},{5,7},{6,4},{7,5},{8,10},{9,11},{10,... | collective-permute-start | bytes 983048 | tf_op jit(solution)/shard_map/ppermute | solution.py:36
  79.3 1.5 copy-start.4
  79.3 7.9 %collective-permute-start.8 = (bf16[320,256]{1,0:T(8,128)(2,1)S(1)}, bf16[320,256]{1,0:T(8,128)(2,1)S(1)}, u32[]{:S(2)}, u32[]{:S(2)}) collective-permute-start(bf16[320,256]{1,0:T(8,128)(2,1)S(1)} %dynamic-slice_convert_fusion.1.refs_0_), channel_id=1, source_target_pairs={{0,4},{1,5},{2,6},{3,7},{4,0},{5,1},{6,2},{7,3},{8,12},{9,13},{10,... | collective-permute-start | bytes 491528 | tf_op jit(solution)/shard_map/ppermute | solution.py:36
  80.8 16.7 %copy-start.10 = (bf16[16,256]{1,0:T(8,128)(2,1)S(1)}, bf16[16,256]{1,0:T(8,128)(2,1)}, u32[]{:S(2)}) copy-start(bf16[16,256]{1,0:T(8,128)(2,1)} %get-tuple-element.26) | copy-start | bytes 24580
  87.9 4.5 %collective-permute-start.9 = (bf16[160,256]{1,0:T(8,128)(2,1)S(1)}, bf16[160,256]{1,0:T(8,128)(2,1)S(1)}, u32[]{:S(2)}, u32[]{:S(2)}) collective-permute-start(bf16[160,256]{1,0:T(8,128)(2,1)S(1)} %dynamic-slice_convert_fusion.2), channel_id=1, source_target_pairs={{0,8},{1,9},{2,10},{3,11},{4,12},{5,13},{6,14},{7,15},{8,0},{9,1},... | collective-permute-start | bytes 245768 | tf_op jit(solution)/shard_map/ppermute | solution.py:36
  92.5 5.0 %collective-permute-start.10 = (bf16[80,256]{1,0:T(8,128)(2,1)S(1)}, bf16[80,256]{1,0:T(8,128)(2,1)S(1)}, u32[]{:S(2)}, u32[]{:S(2)}) collective-permute-start(bf16[80,256]{1,0:T(8,128)(2,1)S(1)} %dynamic-slice_convert_fusion.3), channel_id=1, source_target_pairs={{0,16},{1,17},{2,18},{3,19},{4,20},{5,21},{6,22},{7,23},{8,24},{9,... | collective-permute-start | bytes 122888 | tf_op jit(solution)/shard_map/ppermute | solution.py:36
  97.5 5.3 %collective-permute-start.11 = (bf16[96,256]{1,0:T(8,128)(2,1)S(1)}, bf16[96,256]{1,0:T(8,128)(2,1)S(1)}, u32[]{:S(2)}, u32[]{:S(2)}) collective-permute-start(bf16[96,256]{1,0:T(8,128)(2,1)S(1)} %pad_maximum_fusion.6), channel_id=1, source_target_pairs={{0,16},{1,17},{2,18},{3,19},{4,20},{5,21},{6,22},{7,23},{8,24},{9,... | collective-permute-start | bytes 147464 | tf_op jit(solution)/shard_map/ppermute | solution.py:36
  102.8 4.7 %collective-permute-start.12 = (bf16[192,256]{1,0:T(8,128)(2,1)S(1)}, bf16[192,256]{1,0:T(8,128)(2,1)S(1)}, u32[]{:S(2)}, u32[]{:S(2)}) collective-permute-start(bf16[192,256]{1,0:T(8,128)(2,1)S(1)} %pad_maximum_fusion.4), channel_id=1, source_target_pairs={{0,8},{1,9},{2,10},{3,11},{4,12},{5,13},{6,14},{7,15},{8,0},{9,1},... | collective-permute-start | bytes 294920 | tf_op jit(solution)/shard_map/ppermute | solution.py:36
  107.5 5.7 %collective-permute-start.13 = (bf16[384,256]{1,0:T(8,128)(2,1)S(1)}, bf16[384,256]{1,0:T(8,128)(2,1)S(1)}, u32[]{:S(2)}, u32[]{:S(2)}) collective-permute-start(bf16[384,256]{1,0:T(8,128)(2,1)S(1)} %pad_maximum_fusion.3), channel_id=1, source_target_pairs={{0,4},{1,5},{2,6},{3,7},{4,0},{5,1},{6,2},{7,3},{8,12},{9,13},{10,... | collective-permute-start | bytes 589832 | tf_op jit(solution)/shard_map/ppermute | solution.py:36
  113.4 1.6 %copy-start.2 = (bf16[768,256]{1,0:T(8,128)(2,1)}, bf16[768,256]{1,0:T(8,128)(2,1)S(1)}, u32[]{:S(2)}) copy-start(bf16[768,256]{1,0:T(8,128)(2,1)S(1)} %pad_maximum_fusion.2.refs_0_) | copy-start | bytes 1179652
  113.4 8.8 %collective-permute-start.14 = (bf16[768,256]{1,0:T(8,128)(2,1)S(1)}, bf16[768,256]{1,0:T(8,128)(2,1)S(1)}, u32[]{:S(2)}, u32[]{:S(2)}) collective-permute-start(bf16[768,256]{1,0:T(8,128)(2,1)S(1)} %pad_maximum_fusion.2.refs_0_), channel_id=1, source_target_pairs={{0,2},{1,3},{2,0},{3,1},{4,6},{5,7},{6,4},{7,5},{8,10},{9,11},{10,... | collective-permute-start | bytes 1179656 | tf_op jit(solution)/shard_map/ppermute | solution.py:36
  121.4 1.0 copy-start.11
  121.4 1.2 copy-start.12
  122.4 2.4 %collective-permute-start.15 = (bf16[1536,256]{1,0:T(8,128)(2,1)S(1)}, bf16[1536,256]{1,0:T(8,128)(2,1)S(1)}, u32[]{:S(2)}, u32[]{:S(2)}) collective-permute-start(bf16[1536,256]{1,0:T(8,128)(2,1)S(1)} %pad_maximum_fusion.1), channel_id=1, source_target_pairs={{0,1},{1,0},{2,3},{3,2},{4,5},{5,4},{6,7},{7,6},{8,9},{9,8},{10,11... | collective-permute-start | bytes 2359304 | tf_op jit(solution)/shard_map/ppermute | solution.py:36
  124.7 1.0 copy-start.1
  125.7 11.0 %copy-start = (bf16[128,6144]{1,0:T(8,128)(2,1)S(1)}, bf16[128,6144]{1,0:T(8,128)(2,1)}, u32[]{:S(2)}) copy-start(bf16[128,6144]{1,0:T(8,128)(2,1)} %all_to_all.17.columns_ref) | copy-start | bytes 4718596

commit v3 on v2

--- a/solution.py
+++ b/solution.py
@@ -17,8 +17,7 @@
 AXES = ("gx", "gy")
 BLOCK = 256
 LANES = 128
-PIECES = 3
-PIECES_AT = (1, 2)
+PIECES = (0, 2, 3, 4, 6)
 SMALL = pl.CostEstimate(flops=1, bytes_accessed=1, transcendentals=0)
 F32 = jnp.float32
 BF16 = jnp.bfloat16
@@ -217,12 +216,13 @@
     mark_ref[...] = jnp.zeros_like(mark_ref)
 
 
-def momentum_piece(latent, momentum, columns, after, held, piece, pieces):
+def momentum_piece(latent, momentum, columns, after, held, piece):
     size, count = momentum.shape
     tasks = columns.shape[0]
-    tile = column_tile(count // pieces, 1024)
-    steps = count // pieces // tile
-    first = piece * steps
+    begin, end = [share * count // PIECES[-1] for share in PIECES[piece : piece + 2]]
+    steps = 2
+    tile = (end - begin) // steps
+    first = begin // tile
     anywhere = pl.BlockSpec(memory_space=pl.ANY)
     operands = (latent, momentum, columns, after) + (() if held is None else (held,))
     return pl.pallas_call(
@@ -296,9 +296,8 @@
         spread(d_ref, j, poly)
     for j, rows in upper:
         rest = a * p_ref[rows, part(j)] + product(d_ref, pb_ref, j)
-        spread(xb_ref, j, rest)
-        spread(weight_ref, j, (MOMENTUM_DECAY**2 / whole) * rest)
-    side = (beta / whole) * (a * a * turned.astype(F32) + dot(xb_ref[...], turned))
+        spread(weight_ref, j, (1.0 / (a * a)) * rest)
+    side = (beta / MOMENTUM_DECAY**2) * (turned.astype(F32) + dot(weight_ref[:, :size], turned))
     high = side.astype(BF16)
     weight_ref[:, size : size + tasks] = high
     weight_ref[:, size + tasks :] = (side - high.astype(F32)).astype(BF16)
@@ -401,29 +400,34 @@
     latent, kept, sent, note = blended_gram(side, origin, cross, gram, squares, [held] + far)
 
     new_momentum = None
-    for place, distance in enumerate(distances):
+    for place, distance in enumerate(distances[:-1]):
         if place > 0:
             kept, sent = halves(gram, distance, me)
         got = swap(sent, distance, count)
-        if place in PIECES_AT:
+        if place in (1, 2):
             new_momentum, mark = momentum_piece(
-                latent, momentum, columns, sent, new_momentum, place - PIECES_AT[0], PIECES
+                latent, momentum, columns, sent, new_momentum, place - 1
             )
             kept = kept + mark
         gram = kept + got.astype(F32)
     shard = gram.shape[0]
-    gram = jnp.concatenate([gram.astype(BF16), note], axis=0)
-    for distance in distances[::-1]:
+    sent = jnp.concatenate([gram.astype(BF16), note], axis=0)
+    got = swap(sent, distances[-1], count)
+    gram = (sent[:shard].astype(F32) + got[:shard].astype(F32)).astype(BF16)
+    row = lax.broadcasted_iota(jnp.int32, note.shape, 0)
+    note = jnp.where(row == 0, note, jnp.where(row == 1, got[shard:], jnp.zeros_like(note)))
+    gram = jnp.concatenate([gram, note], axis=0)
+    for place, distance in reversed(list(enumerate(distances[:-1]))):
         got = swap(gram, distance, count)
-        if distance == 2:
+        if place in (1, 2):
             new_momentum, mark = momentum_piece(
-                latent, momentum, columns, gram, new_momentum, PIECES - 1, PIECES
+                latent, momentum, columns, gram, new_momentum, 4 - place
             )
             got = got + mark.astype(BF16)
-        if distance > 1:
+        if place > 0:
             gram = doubled(gram, got, distance, me)
-    apart = [x.reshape(count // 2, -1, BLOCK) for x in (gram, got)]
-    notes = jnp.concatenate([x[:, shard] for x in apart], axis=0)
+    apart = [x.reshape(count // 4, -1, BLOCK) for x in (gram, got)]
+    notes = jnp.concatenate([x[:, shard : shard + 2].reshape(-1, BLOCK) for x in apart], axis=0)
     gram, got = [x[:, :shard].reshape(-1, BLOCK) for x in apart]
     gram = doubled(gram, got, 1, me)
 

time: 162 us -> 156 us (0.963)
  waiting for transfers between devices: 37.4 us -> 28.8 us
  Pallas kernels: 87.3 us -> 90.3 us
    ppermute x16 -> x15, waiting for transfers between devices: 32.6 us -> 24 us  [swap(): return lax.ppermute(x, AXES, [(i, i ^ distance) for i in range(count)])]
    pallas_call x3 -> x4, Pallas kernels: 19.4 us -> 22.4 us  [momentum_piece(): pl.pallas_call(momentum_kernel, grid=(steps,), in_specs=[pl.BlockSpec((ta...]
    ppermute x16 -> x15, starting transfers between devices: 19 us -> 18.5 us  [swap(): return lax.ppermute(x, AXES, [(i, i ^ distance) for i in range(count)])]
  transfers between devices with their start and end apart: 17 -> 16, of which waited for: 11 -> 9; matrix products, arithmetic and copies ran while one was open for 2% -> 2% of each run, Pallas kernels for 29% -> 32%
where the time goes in v3:
time: 156 us
  Pallas kernels  90.3 us (58%)
  waiting for transfers between devices  28.8 us (18%)
  starting transfers between devices  25.8 us (17%)
  other arithmetic  6.6 us (4%)
  local copies, waits for them, and re-layouts  3.15 us (2%)
    pallas_call x1, Pallas kernels, step_pass(): pl.pallas_call(step_kernel, grid=(count // tile,), in_specs=[pl.BlockSpec...  24.4 us
    ppermute x15, waiting for transfers between devices, swap(): return lax.ppermute(x, AXES, [(i, i ^ distance) for i in range(count)])  24 us
    pallas_call x4, Pallas kernels, momentum_piece(): pl.pallas_call(momentum_kernel, grid=(steps,), in_specs=[pl.BlockSpec((ta...  22.4 us
    pallas_call x1, Pallas kernels, gram_pass(): pl.pallas_call(gram_kernel, grid=(count // tile,), in_specs=[pl.BlockSpec...  18.8 us
    ppermute x15, starting transfers between devices, swap(): return lax.ppermute(x, AXES, [(i, i ^ distance) for i in range(count)])  18.5 us
    pallas_call x1, Pallas kernels, poly_pass(): pl.pallas_call(poly_kernel, grid=(1,), in_specs=[entire(x) for x in opera...  11 us
    pallas_call x1, Pallas kernels, cross_pass(): pl.pallas_call(cross_kernel, grid=(count // tile,), in_specs=[pl.BlockSpe...  8.89 us
    all_to_all x1, starting transfers between devices, per_device(): lax.all_to_all(factor_grads, AXES, split_axis=1, concat_axis=0, tiled=True)  7.3 us
  transfers between devices with their start and end apart: 16, of which 9 were waited for; matrix products, arithmetic and copies ran while one was open for 2% of the time, Pallas kernels for 32%

profile of v3, /device:TPU:0, one launch (start us, length us, event | category | flops | bytes accessed | tf_op | source)
XLA Modules:
  0.0 155.6 jit_solution(1337942005233275209)
XLA Ops:
  0.6 7.3 %all-to-all-start = ((bf16[4,32,6144]{2,0,1:T(4,128)(2,1)}), bf16[4,32,6144]{2,0,1:T(4,128)(2,1)S(1)}, u32[]{:S(2)}, u32[]{:S(2)}) async-start(bf16[4,32,6144]{2,0,1:T(4,128)(2,1)} %bitcast.20), calls=%async_computation | async-start | bytes 3145728 | tf_op jit(solution)/shard_map/all_to_all | solution.py:389
  8.0 0.1 copy.19
  8.1 0.1 copy.20
  8.2 0.1 fusion.14
  8.3 0.3 collective-permute-start
  8.6 0.9 collective-permute-done
  9.6 1.8 %collective-permute-start.1 = (bf16[8,1152]{1,0:T(8,128)(2,1)S(1)}, bf16[8,1152]{1,0:T(8,128)(2,1)S(1)}, u32[]{:S(2)}, u32[]{:S(2)}) collective-permute-start(bf16[8,1152]{1,0:T(8,128)(2,1)S(1)} %pad_maximum_fusion.8), channel_id=1, source_target_pairs={{0,2},{1,3},{2,0},{3,1},{4,6},{5,7},{6,4},{7,5},{8,10},{9,11},{10,... | collective-permute-start | bytes 55304 | tf_op jit(solution)/shard_map/ppermute | solution.py:35
  11.4 2.6 %collective-permute-done.1 = bf16[8,1152]{1,0:T(8,128)(2,1)S(1)} collective-permute-done((bf16[8,1152]{1,0:T(8,128)(2,1)S(1)}, bf16[8,1152]{1,0:T(8,128)(2,1)S(1)}, u32[]{:S(2)}, u32[]{:S(2)}) %collective-permute-start.1) | collective-permute-done | bytes 18464 | tf_op jit(solution)/shard_map/ppermute | solution.py:35
  14.0 6.3 %collective-permute-start.2 = (bf16[16,1152]{1,0:T(8,128)(2,1)S(1)}, bf16[16,1152]{1,0:T(8,128)(2,1)S(1)}, u32[]{:S(2)}, u32[]{:S(2)}) collective-permute-start(bf16[16,1152]{1,0:T(8,128)(2,1)S(1)} %pad_maximum_fusion.7), channel_id=1, source_target_pairs={{0,4},{1,5},{2,6},{3,7},{4,0},{5,1},{6,2},{7,3},{8,12},{9,13},{10,... | collective-permute-start | bytes 110600 | tf_op jit(solution)/shard_map/ppermute | solution.py:35
  20.3 0.7 fusion.9.origin_ref
  21.0 18.8 %momentum_gram.1 = (bf16[1024,6144]{1,0:T(8,128)(2,1)}, f32[2560,256]{1,0:T(8,128)}, f32[8,128]{1,0:T(8,128)}) custom-call(f32[1024,6144]{1,0:T(8,128)} %momentum_ref.11), custom_call_target="tpu_custom_call" | custom-call | flops 1 | bytes 1 | tf_op jit(solution)/shard_map/momentum_gram/pallas_call | solution.py:86
  39.9 1.5 collective-permute-start.5
  41.3 0.8 collective-permute-start.4
  42.1 2.2 %collective-permute-start.3 = (bf16[32,1152]{1,0:T(8,128)(2,1)S(1)}, bf16[32,1152]{1,0:T(8,128)(2,1)S(1)}, u32[]{:S(2)}, u32[]{:S(2)}) collective-permute-start(bf16[32,1152]{1,0:T(8,128)(2,1)S(1)} %pad_maximum_fusion.6.refs_0_), channel_id=1, source_target_pairs={{0,8},{1,9},{2,10},{3,11},{4,12},{5,13},{6,14},{7,15},{8,0},{9,1},... | collective-permute-start | bytes 221192 | tf_op jit(solution)/shard_map/ppermute | solution.py:35
  44.3 4.8 %all-to-all-done = bf16[4,32,6144]{2,0,1:T(4,128)(2,1)S(1)} async-done(((bf16[4,32,6144]{2,0,1:T(4,128)(2,1)}), bf16[4,32,6144]{2,0,1:T(4,128)(2,1)S(1)}, u32[]{:S(2)}, u32[]{:S(2)}) %all-to-all-start) | async-done | bytes 1572896 | tf_op jit(solution)/shard_map/all_to_all | solution.py:389
  49.1 1.3 all_to_all.17.columns_ref
  50.4 8.9 %cross_terms.1.cross_ref = f32[128,1152]{1,0:T(8,128)} custom-call(bf16[128,6144]{1,0:T(8,128)(2,1)} %all_to_all.17.columns_ref, bf16[1024,6144]{1,0:T(8,128)(2,1)} %get-tuple-element.19.rounded_ref), custom_call_target="tpu_custom_call" | custom-call | flops 1610612736 | bytes 12582912 | tf_op jit(solution)/shard_map/cross_terms/pallas_call | solution.py:123
  59.3 0.0 collective-permute-done.5.refs_3_
  59.3 0.0 collective-permute-done.4.refs_2_
  59.4 0.6 copy-done.8
  59.9 0.0 copy-done.9
  60.0 0.0 copy-done.10
  60.0 4.8 %blended_gram.1 = (bf16[128,1024]{1,0:T(8,128)(2,1)}, f32[1280,256]{1,0:T(8,128)}, bf16[1280,256]{1,0:T(8,128)(2,1)}, bf16[16,256]{1,0:T(8,128)(2,1)}) custom-call(s32[1]{0:T(128)} %bitcast.side_ref, f32[128,1]{1,0:T(8,128)} %fusion.9.origin_ref, f32[128,1152]{1,0:T(8,128)} %cross_terms.1.cross_ref, f32[2560,256]{1,0:T(8,128)} %get-tuple-element.20.momentum_gram_ref, ...), custom_call_target="tpu_custom_call" | custom-call | flops 536870912 | bytes 5242880 | tf_op jit(solution)/shard_map/blended_gram/pallas_call | solution.py:197
  64.8 0.0 collective-permute-start.6
  64.8 2.3 %collective-permute-done.6 = bf16[1280,256]{1,0:T(8,128)(2,1)S(1)} collective-permute-done((bf16[1280,256]{1,0:T(8,128)(2,1)}, bf16[1280,256]{1,0:T(8,128)(2,1)S(1)}, u32[]{:S(2)}, u32[]{:S(2)}) %collective-permute-start.6) | collective-permute-done | bytes 655392 | tf_op jit(solution)/shard_map/ppermute | solution.py:35
  67.2 1.4 convert_add_fusion
  68.6 0.0 copy-start.3
  68.7 1.1 collective-permute-start.7
  69.8 6.5 %new_momentum.4 = (f32[1024,6144]{1,0:T(8,128)}, f32[1,256]{1,0:T(1,128)}) custom-call(bf16[128,1024]{1,0:T(8,128)(2,1)} %get-tuple-element.22.latent_ref, f32[1024,6144]{1,0:T(8,128)} %momentum_ref.11, bf16[128,6144]{1,0:T(8,128)(2,1)} %all_to_all.17.columns_ref, bf16[640,256]{1,0:T(8,128)(2,1)} %copy-done.3), custom_call_target="tpu_custom_call" | custom-call | flops 1 | bytes 1 | tf_op jit(solution)/shard_map/new_momentum/pallas_call | solution.py:228
  76.2 2.2 %collective-permute-done.7 = bf16[640,256]{1,0:T(8,128)(2,1)S(1)} collective-permute-done((bf16[640,256]{1,0:T(8,128)(2,1)S(1)}, bf16[640,256]{1,0:T(8,128)(2,1)S(1)}, u32[]{:S(2)}, u32[]{:S(2)}) %collective-permute-start.7) | collective-permute-done | bytes 327712 | tf_op jit(solution)/shard_map/ppermute | solution.py:35
  78.5 0.7 convert_add_fusion.1
  79.2 0.0 copy-start.5
  79.3 1.5 collective-permute-start.8
  80.8 4.8 %new_momentum.5 = (f32[1024,6144]{1,0:T(8,128)}, f32[1,256]{1,0:T(1,128)}) custom-call(bf16[128,1024]{1,0:T(8,128)(2,1)} %get-tuple-element.22.latent_ref, f32[1024,6144]{1,0:T(8,128)} %momentum_ref.11, bf16[128,6144]{1,0:T(8,128)(2,1)} %all_to_all.17.columns_ref, bf16[320,256]{1,0:T(8,128)(2,1)} %copy-done.5, ...), custom_call_target="tpu_custom_call", output_to_operand_aliasing={{0}: (4, {})} | custom-call | flops 1 | bytes 1 | tf_op jit(solution)/shard_map/new_momentum/pallas_call | solution.py:228
  85.5 0.0 collective-permute-done.8
  85.5 0.7 convert_add_fusion.2
  86.2 0.1 collective-permute-start.9
  86.3 4.4 %collective-permute-done.9 = bf16[160,256]{1,0:T(8,128)(2,1)S(1)} collective-permute-done((bf16[160,256]{1,0:T(8,128)(2,1)S(1)}, bf16[160,256]{1,0:T(8,128)(2,1)S(1)}, u32[]{:S(2)}, u32[]{:S(2)}) %collective-permute-start.9) | collective-permute-done | bytes 81952 | tf_op jit(solution)/shard_map/ppermute | solution.py:35
  90.8 0.1 collective-permute-start.10
  90.9 5.8 %collective-permute-done.10 = bf16[176,256]{1,0:T(8,128)(2,1)S(1)} collective-permute-done((bf16[176,256]{1,0:T(8,128)(2,1)S(1)}, bf16[176,256]{1,0:T(8,128)(2,1)S(1)}, u32[]{:S(2)}, u32[]{:S(2)}) %collective-permute-start.10) | collective-permute-done | bytes 90144 | tf_op jit(solution)/shard_map/ppermute | solution.py:35
  96.7 0.1 fusion.11
  96.8 0.1 collective-permute-start.11
  96.9 4.5 %collective-permute-done.11 = bf16[176,256]{1,0:T(8,128)(2,1)S(1)} collective-permute-done((bf16[176,256]{1,0:T(8,128)(2,1)S(1)}, bf16[176,256]{1,0:T(8,128)(2,1)S(1)}, u32[]{:S(2)}, u32[]{:S(2)}) %collective-permute-start.11) | collective-permute-done | bytes 90144 | tf_op jit(solution)/shard_map/ppermute | solution.py:35
  101.5 0.0 copy-start.4
  101.5 0.8 collective-permute-start.12
  102.3 4.7 %new_momentum.6 = (f32[1024,6144]{1,0:T(8,128)}, f32[1,256]{1,0:T(1,128)}) custom-call(bf16[128,1024]{1,0:T(8,128)(2,1)} %get-tuple-element.22.latent_ref, f32[1024,6144]{1,0:T(8,128)} %momentum_ref.11, bf16[128,6144]{1,0:T(8,128)(2,1)} %all_to_all.17.columns_ref, bf16[352,256]{1,0:T(8,128)(2,1)} %copy-done.4, ...), custom_call_target="tpu_custom_call", output_to_operand_aliasing={{0}: (4, {})} | custom-call | flops 1 | bytes 1 | tf_op jit(solution)/shard_map/new_momentum/pallas_call | solution.py:228
  107.0 0.7 convert_reduce_fusion.1
  107.7 0.0 collective-permute-done.12
  107.7 0.1 broadcast_select_fusion.5
  107.8 0.0 copy-start.2
  107.9 1.8 %collective-permute-start.13 = (bf16[704,256]{1,0:T(8,128)(2,1)S(1)}, bf16[704,256]{1,0:T(8,128)(2,1)S(1)}, u32[]{:S(2)}, u32[]{:S(2)}) collective-permute-start(bf16[704,256]{1,0:T(8,128)(2,1)S(1)} %pad_maximum_fusion.2.refs_0_), channel_id=1, source_target_pairs={{0,2},{1,3},{2,0},{3,1},{4,6},{5,7},{6,4},{7,5},{8,10},{9,11},{10,... | collective-permute-start | bytes 1081352 | tf_op jit(solution)/shard_map/ppermute | solution.py:35
  109.7 6.4 %new_momentum.7 = (f32[1024,6144]{1,0:T(8,128)}, f32[1,256]{1,0:T(1,128)}) custom-call(bf16[128,1024]{1,0:T(8,128)(2,1)} %get-tuple-element.22.latent_ref, f32[1024,6144]{1,0:T(8,128)} %momentum_ref.11, bf16[128,6144]{1,0:T(8,128)(2,1)} %all_to_all.17.columns_ref, bf16[704,256]{1,0:T(8,128)(2,1)} %copy-done.2, ...), custom_call_target="tpu_custom_call", output_to_operand_aliasing={{0}: (4, {})} | custom-call | flops 1 | bytes 1 | tf_op jit(solution)/shard_map/new_momentum/pallas_call | solution.py:228
  116.1 0.7 convert_reduce_fusion
  116.8 0.1 broadcast_select_fusion.3
  117.0 0.1 collective-permute-start.14
  117.1 0.1 slice.25
  117.2 0.1 pad_add_fusion
  117.3 0.8 select_reduce_fusion
  118.1 1.2 collective-permute-done.14
  119.3 0.1 broadcast_select_fusion.1
  119.4 0.1 pad_maximum_fusion.gram_ref
  119.5 0.7 copy-done.1
  120.3 11.0 %polynomial.1 = (bf16[1024,1280]{1,0:T(8,128)(2,1)}, f32[1,6144]{1,0:T(1,128)S(1)}) custom-call(bf16[32,256]{1,0:T(8,128)(2,1)S(1)} %pad_maximum_fusion.9.notes_ref, f32[1,6144]{1,0:T(1,128)S(1)} %bitcast.14, bf16[2560,256]{1,0:T(8,128)(2,1)S(1)} %pad_maximum_fusion.gram_ref, bf16[128,1024]{1,0:T(8,128)(2,1)S(1)} %copy-done.1), custom_call_target="tpu_custom_call" | custom-call | flops 10737418240 | bytes 4194304 | tf_op jit(solution)/shard_map/polynomial/pallas_call | solution.py:313
  131.2 24.4 %step.1 = f32[1024,6144]{1,0:T(8,128)} custom-call(bf16[1024,1280]{1,0:T(8,128)(2,1)} %get-tuple-element.34.weight_ref, f32[1,6144]{1,0:T(1,128)S(1)} %get-tuple-element.35.factor_ref, f32[1024,6144]{1,0:T(8,128)} %momentum_ref.11, bf16[128,6144]{1,0:T(8,128)(2,1)S(1)} %copy-done), custom_call_target="tpu_custom_call" | custom-call | flops 16106127360 | bytes 50331648 | tf_op jit(solution)/shard_map/step/pallas_call | solution.py:348
  (49 shorter events, 0.5 us)
Async XLA Ops:
  0.6 7.3 %copy-start.14 = (s32[4]{0:T(128)S(1)}, s32[4]{0:T(128)}, u32[]{:S(2)}) copy-start(s32[4]{0:T(128)} %param.8) | copy-start | bytes 52
  0.6 7.6 %copy-start.7 = (bf16[4,1024]{1,0:T(4,128)(2,1)S(1)}, bf16[4,1024]{1,0:T(4,128)(2,1)}, u32[]{:S(2)}) copy-start(bf16[4,1024]{1,0:T(4,128)(2,1)} %param.7) | copy-start | bytes 24580
  0.6 48.5 %all-to-all-start = ((bf16[4,32,6144]{2,0,1:T(4,128)(2,1)}), bf16[4,32,6144]{2,0,1:T(4,128)(2,1)S(1)}, u32[]{:S(2)}, u32[]{:S(2)}) async-start(bf16[4,32,6144]{2,0,1:T(4,128)(2,1)} %bitcast.20), calls=%async_computation | async-start | bytes 3145728 | tf_op jit(solution)/shard_map/all_to_all | solution.py:389
  8.3 1.2 collective-permute-start
  9.6 4.4 %collective-permute-start.1 = (bf16[8,1152]{1,0:T(8,128)(2,1)S(1)}, bf16[8,1152]{1,0:T(8,128)(2,1)S(1)}, u32[]{:S(2)}, u32[]{:S(2)}) collective-permute-start(bf16[8,1152]{1,0:T(8,128)(2,1)S(1)} %pad_maximum_fusion.8), channel_id=1, source_target_pairs={{0,2},{1,3},{2,0},{3,1},{4,6},{5,7},{6,4},{7,5},{8,10},{9,11},{10,... | collective-permute-start | bytes 55304 | tf_op jit(solution)/shard_map/ppermute | solution.py:35
  14.0 25.8 %collective-permute-start.2 = (bf16[16,1152]{1,0:T(8,128)(2,1)S(1)}, bf16[16,1152]{1,0:T(8,128)(2,1)S(1)}, u32[]{:S(2)}, u32[]{:S(2)}) collective-permute-start(bf16[16,1152]{1,0:T(8,128)(2,1)S(1)} %pad_maximum_fusion.7), channel_id=1, source_target_pairs={{0,4},{1,5},{2,6},{3,7},{4,0},{5,1},{6,2},{7,3},{8,12},{9,13},{10,... | collective-permute-start | bytes 110600 | tf_op jit(solution)/shard_map/ppermute | solution.py:35
  39.8 19.5 %copy-start.6 = (bf16[32,1152]{1,0:T(8,128)(2,1)}, bf16[32,1152]{1,0:T(8,128)(2,1)S(1)}, u32[]{:S(2)}) copy-start(bf16[32,1152]{1,0:T(8,128)(2,1)S(1)} %pad_maximum_fusion.6.refs_0_) | copy-start | bytes 221188
  39.9 19.5 %collective-permute-start.5 = (bf16[32,1152]{1,0:T(8,128)(2,1)S(1)}, bf16[32,1152]{1,0:T(8,128)(2,1)S(1)}, u32[]{:S(2)}, u32[]{:S(2)}) collective-permute-start(bf16[32,1152]{1,0:T(8,128)(2,1)S(1)} %pad_maximum_fusion.6.refs_0_), channel_id=1, source_target_pairs={{0,24},{1,25},{2,26},{3,27},{4,28},{5,29},{6,30},{7,31},{8,16},{9,... | collective-permute-start | bytes 221192 | tf_op jit(solution)/shard_map/ppermute | solution.py:35
  41.3 18.0 %collective-permute-start.4 = (bf16[32,1152]{1,0:T(8,128)(2,1)S(1)}, bf16[32,1152]{1,0:T(8,128)(2,1)S(1)}, u32[]{:S(2)}, u32[]{:S(2)}) collective-permute-start(bf16[32,1152]{1,0:T(8,128)(2,1)S(1)} %pad_maximum_fusion.6.refs_0_), channel_id=1, source_target_pairs={{0,16},{1,17},{2,18},{3,19},{4,20},{5,21},{6,22},{7,23},{8,24},{9,... | collective-permute-start | bytes 221192 | tf_op jit(solution)/shard_map/ppermute | solution.py:35
  42.1 17.3 %collective-permute-start.3 = (bf16[32,1152]{1,0:T(8,128)(2,1)S(1)}, bf16[32,1152]{1,0:T(8,128)(2,1)S(1)}, u32[]{:S(2)}, u32[]{:S(2)}) collective-permute-start(bf16[32,1152]{1,0:T(8,128)(2,1)S(1)} %pad_maximum_fusion.6.refs_0_), channel_id=1, source_target_pairs={{0,8},{1,9},{2,10},{3,11},{4,12},{5,13},{6,14},{7,15},{8,0},{9,1},... | collective-permute-start | bytes 221192 | tf_op jit(solution)/shard_map/ppermute | solution.py:35
  59.3 0.6 copy-start.8
  59.3 0.6 copy-start.9
  59.4 0.6 copy-start.10
  64.8 2.3 %collective-permute-start.6 = (bf16[1280,256]{1,0:T(8,128)(2,1)}, bf16[1280,256]{1,0:T(8,128)(2,1)S(1)}, u32[]{:S(2)}, u32[]{:S(2)}) collective-permute-start(bf16[1280,256]{1,0:T(8,128)(2,1)} %get-tuple-element.24), channel_id=1, source_target_pairs={{0,1},{1,0},{2,3},{3,2},{4,5},{5,4},{6,7},{7,6},{8,9},{9,8},{10,11... | collective-permute-start | bytes 1966088 | tf_op jit(solution)/shard_map/ppermute | solution.py:35
  68.6 1.1 copy-start.3
  68.7 9.8 %collective-permute-start.7 = (bf16[640,256]{1,0:T(8,128)(2,1)S(1)}, bf16[640,256]{1,0:T(8,128)(2,1)S(1)}, u32[]{:S(2)}, u32[]{:S(2)}) collective-permute-start(bf16[640,256]{1,0:T(8,128)(2,1)S(1)} %dynamic-slice_convert_fusion.refs_0_), channel_id=1, source_target_pairs={{0,2},{1,3},{2,0},{3,1},{4,6},{5,7},{6,4},{7,5},{8,10},{9,11},{10,... | collective-permute-start | bytes 983048 | tf_op jit(solution)/shard_map/ppermute | solution.py:35
  79.2 1.5 copy-start.5
  79.3 6.2 %collective-permute-start.8 = (bf16[320,256]{1,0:T(8,128)(2,1)S(1)}, bf16[320,256]{1,0:T(8,128)(2,1)S(1)}, u32[]{:S(2)}, u32[]{:S(2)}) collective-permute-start(bf16[320,256]{1,0:T(8,128)(2,1)S(1)} %dynamic-slice_convert_fusion.1.refs_0_), channel_id=1, source_target_pairs={{0,4},{1,5},{2,6},{3,7},{4,0},{5,1},{6,2},{7,3},{8,12},{9,13},{10,... | collective-permute-start | bytes 491528 | tf_op jit(solution)/shard_map/ppermute | solution.py:35
  80.8 10.0 %copy-start.11 = (bf16[16,256]{1,0:T(8,128)(2,1)S(1)}, bf16[16,256]{1,0:T(8,128)(2,1)}, u32[]{:S(2)}) copy-start(bf16[16,256]{1,0:T(8,128)(2,1)} %get-tuple-element.28) | copy-start | bytes 24580
  86.2 4.5 %collective-permute-start.9 = (bf16[160,256]{1,0:T(8,128)(2,1)S(1)}, bf16[160,256]{1,0:T(8,128)(2,1)S(1)}, u32[]{:S(2)}, u32[]{:S(2)}) collective-permute-start(bf16[160,256]{1,0:T(8,128)(2,1)S(1)} %dynamic-slice_convert_fusion.2), channel_id=1, source_target_pairs={{0,8},{1,9},{2,10},{3,11},{4,12},{5,13},{6,14},{7,15},{8,0},{9,1},... | collective-permute-start | bytes 245768 | tf_op jit(solution)/shard_map/ppermute | solution.py:35
  90.8 5.9 %collective-permute-start.10 = (bf16[176,256]{1,0:T(8,128)(2,1)S(1)}, bf16[176,256]{1,0:T(8,128)(2,1)S(1)}, u32[]{:S(2)}, u32[]{:S(2)}) collective-permute-start(bf16[176,256]{1,0:T(8,128)(2,1)S(1)} %pad_maximum_fusion.4), channel_id=1, source_target_pairs={{0,16},{1,17},{2,18},{3,19},{4,20},{5,21},{6,22},{7,23},{8,24},{9,... | collective-permute-start | bytes 270344 | tf_op jit(solution)/shard_map/ppermute | solution.py:35
  96.8 4.6 %collective-permute-start.11 = (bf16[176,256]{1,0:T(8,128)(2,1)S(1)}, bf16[176,256]{1,0:T(8,128)(2,1)S(1)}, u32[]{:S(2)}, u32[]{:S(2)}) collective-permute-start(bf16[176,256]{1,0:T(8,128)(2,1)S(1)} %pad_maximum_fusion.5), channel_id=1, source_target_pairs={{0,8},{1,9},{2,10},{3,11},{4,12},{5,13},{6,14},{7,15},{8,0},{9,1},... | collective-permute-start | bytes 270344 | tf_op jit(solution)/shard_map/ppermute | solution.py:35
  101.5 0.8 copy-start.4
  101.5 6.2 %collective-permute-start.12 = (bf16[352,256]{1,0:T(8,128)(2,1)S(1)}, bf16[352,256]{1,0:T(8,128)(2,1)S(1)}, u32[]{:S(2)}, u32[]{:S(2)}) collective-permute-start(bf16[352,256]{1,0:T(8,128)(2,1)S(1)} %pad_maximum_fusion.3.refs_0_), channel_id=1, source_target_pairs={{0,4},{1,5},{2,6},{3,7},{4,0},{5,1},{6,2},{7,3},{8,12},{9,13},{10,... | collective-permute-start | bytes 540680 | tf_op jit(solution)/shard_map/ppermute | solution.py:35
  107.8 1.8 %copy-start.2 = (bf16[704,256]{1,0:T(8,128)(2,1)}, bf16[704,256]{1,0:T(8,128)(2,1)S(1)}, u32[]{:S(2)}) copy-start(bf16[704,256]{1,0:T(8,128)(2,1)S(1)} %pad_maximum_fusion.2.refs_0_) | copy-start | bytes 1081348
  107.9 9.0 %collective-permute-start.13 = (bf16[704,256]{1,0:T(8,128)(2,1)S(1)}, bf16[704,256]{1,0:T(8,128)(2,1)S(1)}, u32[]{:S(2)}, u32[]{:S(2)}) collective-permute-start(bf16[704,256]{1,0:T(8,128)(2,1)S(1)} %pad_maximum_fusion.2.refs_0_), channel_id=1, source_target_pairs={{0,2},{1,3},{2,0},{3,1},{4,6},{5,7},{6,4},{7,5},{8,10},{9,11},{10,... | collective-permute-start | bytes 1081352 | tf_op jit(solution)/shard_map/ppermute | solution.py:35
  116.1 1.0 copy-start.12
  116.1 1.2 copy-start.13
  117.0 2.3 %collective-permute-start.14 = (bf16[1408,256]{1,0:T(8,128)(2,1)S(1)}, bf16[1408,256]{1,0:T(8,128)(2,1)S(1)}, u32[]{:S(2)}, u32[]{:S(2)}) collective-permute-start(bf16[1408,256]{1,0:T(8,128)(2,1)S(1)} %pad_maximum_fusion.1), channel_id=1, source_target_pairs={{0,1},{1,0},{2,3},{3,2},{4,5},{5,4},{6,7},{7,6},{8,9},{9,8},{10,11... | collective-permute-start | bytes 2162696 | tf_op jit(solution)/shard_map/ppermute | solution.py:35
  119.3 1.0 copy-start.1
  120.3 11.0 %copy-start = (bf16[128,6144]{1,0:T(8,128)(2,1)S(1)}, bf16[128,6144]{1,0:T(8,128)(2,1)}, u32[]{:S(2)}) copy-start(bf16[128,6144]{1,0:T(8,128)(2,1)} %all_to_all.17.columns_ref) | copy-start | bytes 4718596

commit v4 on v3

--- a/solution.py
+++ b/solution.py
@@ -119,7 +119,7 @@
 def cross_pass(columns, rounded):
     size, count = rounded.shape
     tasks = columns.shape[0]
-    tile = column_tile(count, 2048)
+    tile = column_tile(count, 3072)
     return pl.pallas_call(
         cross_kernel,
         grid=(count // tile,),

time: 156 us -> 156 us (level)
  no operation moved by 1% of the time
where the time goes in v4:
time: 156 us; the launch traced here: 155 us
  Pallas kernels  90.1 us (58%)
  waiting for transfers between devices  28.8 us (18%)
  starting transfers between devices  25.8 us (17%)
  other arithmetic  6.6 us (4%)
  local copies, waits for them, and re-layouts  3.15 us (2%)
    pallas_call x1, Pallas kernels, step_pass(): pl.pallas_call(step_kernel, grid=(count // tile,), in_specs=[pl.BlockSpec...  24.4 us
    ppermute x15, waiting for transfers between devices, swap(): return lax.ppermute(x, AXES, [(i, i ^ distance) for i in range(count)])  24 us
    pallas_call x4, Pallas kernels, momentum_piece(): pl.pallas_call(momentum_kernel, grid=(steps,), in_specs=[pl.BlockSpec((ta...  22.4 us
    pallas_call x1, Pallas kernels, gram_pass(): pl.pallas_call(gram_kernel, grid=(count // tile,), in_specs=[pl.BlockSpec...  18.8 us
    ppermute x15, starting transfers between devices, swap(): return lax.ppermute(x, AXES, [(i, i ^ distance) for i in range(count)])  18.5 us
    pallas_call x1, Pallas kernels, poly_pass(): pl.pallas_call(poly_kernel, grid=(1,), in_specs=[entire(x) for x in opera...  11 us
    pallas_call x1, Pallas kernels, cross_pass(): pl.pallas_call(cross_kernel, grid=(count // tile,), in_specs=[pl.BlockSpe...  8.73 us
    all_to_all x1, starting transfers between devices, per_device(): lax.all_to_all(factor_grads, AXES, split_axis=1, concat_axis=0, tiled=True)  7.3 us
  transfers between devices with their start and end apart: 16, of which 9 were waited for; matrix products, arithmetic and copies ran while one was open for 2% of the time, Pallas kernels for 32%

profile of v4, /device:TPU:0, one launch (start us, length us, event | category | flops | bytes accessed | tf_op | source)
XLA Modules:
  0.0 155.5 jit_solution(33387480759660928)
XLA Ops:
  0.6 7.3 %all-to-all-start = ((bf16[4,32,6144]{2,0,1:T(4,128)(2,1)}), bf16[4,32,6144]{2,0,1:T(4,128)(2,1)S(1)}, u32[]{:S(2)}, u32[]{:S(2)}) async-start(bf16[4,32,6144]{2,0,1:T(4,128)(2,1)} %bitcast.20), calls=%async_computation | async-start | bytes 3145728 | tf_op jit(solution)/shard_map/all_to_all | solution.py:389
  8.0 0.1 copy.19
  8.1 0.1 copy.20
  8.2 0.1 fusion.14
  8.3 0.3 collective-permute-start
  8.6 0.9 collective-permute-done
  9.6 1.8 %collective-permute-start.1 = (bf16[8,1152]{1,0:T(8,128)(2,1)S(1)}, bf16[8,1152]{1,0:T(8,128)(2,1)S(1)}, u32[]{:S(2)}, u32[]{:S(2)}) collective-permute-start(bf16[8,1152]{1,0:T(8,128)(2,1)S(1)} %pad_maximum_fusion.8), channel_id=1, source_target_pairs={{0,2},{1,3},{2,0},{3,1},{4,6},{5,7},{6,4},{7,5},{8,10},{9,11},{10,... | collective-permute-start | bytes 55304 | tf_op jit(solution)/shard_map/ppermute | solution.py:35
  11.4 2.6 %collective-permute-done.1 = bf16[8,1152]{1,0:T(8,128)(2,1)S(1)} collective-permute-done((bf16[8,1152]{1,0:T(8,128)(2,1)S(1)}, bf16[8,1152]{1,0:T(8,128)(2,1)S(1)}, u32[]{:S(2)}, u32[]{:S(2)}) %collective-permute-start.1) | collective-permute-done | bytes 18464 | tf_op jit(solution)/shard_map/ppermute | solution.py:35
  14.0 6.3 %collective-permute-start.2 = (bf16[16,1152]{1,0:T(8,128)(2,1)S(1)}, bf16[16,1152]{1,0:T(8,128)(2,1)S(1)}, u32[]{:S(2)}, u32[]{:S(2)}) collective-permute-start(bf16[16,1152]{1,0:T(8,128)(2,1)S(1)} %pad_maximum_fusion.7), channel_id=1, source_target_pairs={{0,4},{1,5},{2,6},{3,7},{4,0},{5,1},{6,2},{7,3},{8,12},{9,13},{10,... | collective-permute-start | bytes 110600 | tf_op jit(solution)/shard_map/ppermute | solution.py:35
  20.3 0.7 fusion.9.origin_ref
  21.0 18.8 %momentum_gram.1 = (bf16[1024,6144]{1,0:T(8,128)(2,1)}, f32[2560,256]{1,0:T(8,128)}, f32[8,128]{1,0:T(8,128)}) custom-call(f32[1024,6144]{1,0:T(8,128)} %momentum_ref.11), custom_call_target="tpu_custom_call" | custom-call | flops 1 | bytes 1 | tf_op jit(solution)/shard_map/momentum_gram/pallas_call | solution.py:86
  39.8 0.0 collective-permute-done.2
  39.9 1.5 collective-permute-start.5
  41.3 0.8 collective-permute-start.4
  42.1 2.2 %collective-permute-start.3 = (bf16[32,1152]{1,0:T(8,128)(2,1)S(1)}, bf16[32,1152]{1,0:T(8,128)(2,1)S(1)}, u32[]{:S(2)}, u32[]{:S(2)}) collective-permute-start(bf16[32,1152]{1,0:T(8,128)(2,1)S(1)} %pad_maximum_fusion.6.refs_0_), channel_id=1, source_target_pairs={{0,8},{1,9},{2,10},{3,11},{4,12},{5,13},{6,14},{7,15},{8,0},{9,1},... | collective-permute-start | bytes 221192 | tf_op jit(solution)/shard_map/ppermute | solution.py:35
  44.3 4.8 %all-to-all-done = bf16[4,32,6144]{2,0,1:T(4,128)(2,1)S(1)} async-done(((bf16[4,32,6144]{2,0,1:T(4,128)(2,1)}), bf16[4,32,6144]{2,0,1:T(4,128)(2,1)S(1)}, u32[]{:S(2)}, u32[]{:S(2)}) %all-to-all-start) | async-done | bytes 1572896 | tf_op jit(solution)/shard_map/all_to_all | solution.py:389
  49.1 1.3 all_to_all.17.columns_ref
  50.4 8.7 %cross_terms.1.cross_ref = f32[128,1152]{1,0:T(8,128)} custom-call(bf16[128,6144]{1,0:T(8,128)(2,1)} %all_to_all.17.columns_ref, bf16[1024,6144]{1,0:T(8,128)(2,1)} %get-tuple-element.19.rounded_ref), custom_call_target="tpu_custom_call" | custom-call | flops 1610612736 | bytes 12582912 | tf_op jit(solution)/shard_map/cross_terms/pallas_call | solution.py:123
  59.2 0.0 collective-permute-done.5.refs_3_
  59.2 0.0 collective-permute-done.3.refs_1_
  59.2 0.6 copy-done.8
  59.8 0.0 copy-done.9
  59.8 0.0 copy-done.10
  59.8 4.8 %blended_gram.1 = (bf16[128,1024]{1,0:T(8,128)(2,1)}, f32[1280,256]{1,0:T(8,128)}, bf16[1280,256]{1,0:T(8,128)(2,1)}, bf16[16,256]{1,0:T(8,128)(2,1)}) custom-call(s32[1]{0:T(128)} %bitcast.side_ref, f32[128,1]{1,0:T(8,128)} %fusion.9.origin_ref, f32[128,1152]{1,0:T(8,128)} %cross_terms.1.cross_ref, f32[2560,256]{1,0:T(8,128)} %get-tuple-element.20.momentum_gram_ref, ...), custom_call_target="tpu_custom_call" | custom-call | flops 536870912 | bytes 5242880 | tf_op jit(solution)/shard_map/blended_gram/pallas_call | solution.py:197
  64.7 2.3 %collective-permute-done.6 = bf16[1280,256]{1,0:T(8,128)(2,1)S(1)} collective-permute-done((bf16[1280,256]{1,0:T(8,128)(2,1)}, bf16[1280,256]{1,0:T(8,128)(2,1)S(1)}, u32[]{:S(2)}, u32[]{:S(2)}) %collective-permute-start.6) | collective-permute-done | bytes 655392 | tf_op jit(solution)/shard_map/ppermute | solution.py:35
  67.0 1.4 convert_add_fusion
  68.5 0.0 copy-start.3
  68.5 1.1 collective-permute-start.7
  69.6 6.5 %new_momentum.4 = (f32[1024,6144]{1,0:T(8,128)}, f32[1,256]{1,0:T(1,128)}) custom-call(bf16[128,1024]{1,0:T(8,128)(2,1)} %get-tuple-element.22.latent_ref, f32[1024,6144]{1,0:T(8,128)} %momentum_ref.11, bf16[128,6144]{1,0:T(8,128)(2,1)} %all_to_all.17.columns_ref, bf16[640,256]{1,0:T(8,128)(2,1)} %copy-done.3), custom_call_target="tpu_custom_call" | custom-call | flops 1 | bytes 1 | tf_op jit(solution)/shard_map/new_momentum/pallas_call | solution.py:228
  76.1 2.2 %collective-permute-done.7 = bf16[640,256]{1,0:T(8,128)(2,1)S(1)} collective-permute-done((bf16[640,256]{1,0:T(8,128)(2,1)S(1)}, bf16[640,256]{1,0:T(8,128)(2,1)S(1)}, u32[]{:S(2)}, u32[]{:S(2)}) %collective-permute-start.7) | collective-permute-done | bytes 327712 | tf_op jit(solution)/shard_map/ppermute | solution.py:35
  78.3 0.7 convert_add_fusion.1
  79.1 0.0 copy-start.5
  79.1 1.5 collective-permute-start.8
  80.6 4.8 %new_momentum.5 = (f32[1024,6144]{1,0:T(8,128)}, f32[1,256]{1,0:T(1,128)}) custom-call(bf16[128,1024]{1,0:T(8,128)(2,1)} %get-tuple-element.22.latent_ref, f32[1024,6144]{1,0:T(8,128)} %momentum_ref.11, bf16[128,6144]{1,0:T(8,128)(2,1)} %all_to_all.17.columns_ref, bf16[320,256]{1,0:T(8,128)(2,1)} %copy-done.5, ...), custom_call_target="tpu_custom_call", output_to_operand_aliasing={{0}: (4, {})} | custom-call | flops 1 | bytes 1 | tf_op jit(solution)/shard_map/new_momentum/pallas_call | solution.py:228
  85.4 0.7 convert_add_fusion.2
  86.1 0.1 collective-permute-start.9
  86.2 4.4 %collective-permute-done.9 = bf16[160,256]{1,0:T(8,128)(2,1)S(1)} collective-permute-done((bf16[160,256]{1,0:T(8,128)(2,1)S(1)}, bf16[160,256]{1,0:T(8,128)(2,1)S(1)}, u32[]{:S(2)}, u32[]{:S(2)}) %collective-permute-start.9) | collective-permute-done | bytes 81952 | tf_op jit(solution)/shard_map/ppermute | solution.py:35
  90.6 0.1 collective-permute-start.10
  90.7 5.8 %collective-permute-done.10 = bf16[176,256]{1,0:T(8,128)(2,1)S(1)} collective-permute-done((bf16[176,256]{1,0:T(8,128)(2,1)S(1)}, bf16[176,256]{1,0:T(8,128)(2,1)S(1)}, u32[]{:S(2)}, u32[]{:S(2)}) %collective-permute-start.10) | collective-permute-done | bytes 90144 | tf_op jit(solution)/shard_map/ppermute | solution.py:35
  96.6 0.1 fusion.11
  96.7 0.1 collective-permute-start.11
  96.8 4.5 %collective-permute-done.11 = bf16[176,256]{1,0:T(8,128)(2,1)S(1)} collective-permute-done((bf16[176,256]{1,0:T(8,128)(2,1)S(1)}, bf16[176,256]{1,0:T(8,128)(2,1)S(1)}, u32[]{:S(2)}, u32[]{:S(2)}) %collective-permute-start.11) | collective-permute-done | bytes 90144 | tf_op jit(solution)/shard_map/ppermute | solution.py:35
  101.3 0.0 copy-start.4
  101.3 0.8 collective-permute-start.12
  102.1 4.7 %new_momentum.6 = (f32[1024,6144]{1,0:T(8,128)}, f32[1,256]{1,0:T(1,128)}) custom-call(bf16[128,1024]{1,0:T(8,128)(2,1)} %get-tuple-element.22.latent_ref, f32[1024,6144]{1,0:T(8,128)} %momentum_ref.11, bf16[128,6144]{1,0:T(8,128)(2,1)} %all_to_all.17.columns_ref, bf16[352,256]{1,0:T(8,128)(2,1)} %copy-done.4, ...), custom_call_target="tpu_custom_call", output_to_operand_aliasing={{0}: (4, {})} | custom-call | flops 1 | bytes 1 | tf_op jit(solution)/shard_map/new_momentum/pallas_call | solution.py:228
  106.9 0.7 convert_reduce_fusion.1
  107.6 0.0 collective-permute-done.12
  107.6 0.1 broadcast_select_fusion.5
  107.7 0.0 copy-start.2
  107.7 1.8 %collective-permute-start.13 = (bf16[704,256]{1,0:T(8,128)(2,1)S(1)}, bf16[704,256]{1,0:T(8,128)(2,1)S(1)}, u32[]{:S(2)}, u32[]{:S(2)}) collective-permute-start(bf16[704,256]{1,0:T(8,128)(2,1)S(1)} %pad_maximum_fusion.2.refs_0_), channel_id=1, source_target_pairs={{0,2},{1,3},{2,0},{3,1},{4,6},{5,7},{6,4},{7,5},{8,10},{9,11},{10,... | collective-permute-start | bytes 1081352 | tf_op jit(solution)/shard_map/ppermute | solution.py:35
  109.5 6.4 %new_momentum.7 = (f32[1024,6144]{1,0:T(8,128)}, f32[1,256]{1,0:T(1,128)}) custom-call(bf16[128,1024]{1,0:T(8,128)(2,1)} %get-tuple-element.22.latent_ref, f32[1024,6144]{1,0:T(8,128)} %momentum_ref.11, bf16[128,6144]{1,0:T(8,128)(2,1)} %all_to_all.17.columns_ref, bf16[704,256]{1,0:T(8,128)(2,1)} %copy-done.2, ...), custom_call_target="tpu_custom_call", output_to_operand_aliasing={{0}: (4, {})} | custom-call | flops 1 | bytes 1 | tf_op jit(solution)/shard_map/new_momentum/pallas_call | solution.py:228
  116.0 0.7 convert_reduce_fusion
  116.7 0.0 collective-permute-done.13
  116.7 0.1 broadcast_select_fusion.3
  116.9 0.1 collective-permute-start.14
  117.0 0.1 slice.25
  117.1 0.1 pad_add_fusion
  117.2 0.8 select_reduce_fusion
  118.0 1.2 collective-permute-done.14
  119.2 0.1 broadcast_select_fusion.1
  119.3 0.1 pad_maximum_fusion.gram_ref
  119.4 0.7 copy-done.1
  120.1 11.0 %polynomial.1 = (bf16[1024,1280]{1,0:T(8,128)(2,1)}, f32[1,6144]{1,0:T(1,128)S(1)}) custom-call(bf16[32,256]{1,0:T(8,128)(2,1)S(1)} %pad_maximum_fusion.9.notes_ref, f32[1,6144]{1,0:T(1,128)S(1)} %bitcast.14, bf16[2560,256]{1,0:T(8,128)(2,1)S(1)} %pad_maximum_fusion.gram_ref, bf16[128,1024]{1,0:T(8,128)(2,1)S(1)} %copy-done.1), custom_call_target="tpu_custom_call" | custom-call | flops 10737418240 | bytes 4194304 | tf_op jit(solution)/shard_map/polynomial/pallas_call | solution.py:313
  131.1 24.4 %step.1 = f32[1024,6144]{1,0:T(8,128)} custom-call(bf16[1024,1280]{1,0:T(8,128)(2,1)} %get-tuple-element.34.weight_ref, f32[1,6144]{1,0:T(1,128)S(1)} %get-tuple-element.35.factor_ref, f32[1024,6144]{1,0:T(8,128)} %momentum_ref.11, bf16[128,6144]{1,0:T(8,128)(2,1)S(1)} %copy-done), custom_call_target="tpu_custom_call" | custom-call | flops 16106127360 | bytes 50331648 | tf_op jit(solution)/shard_map/step/pallas_call | solution.py:348
  (49 shorter events, 0.5 us)
Async XLA Ops:
  0.6 7.3 %copy-start.14 = (s32[4]{0:T(128)S(1)}, s32[4]{0:T(128)}, u32[]{:S(2)}) copy-start(s32[4]{0:T(128)} %param.8) | copy-start | bytes 52
  0.6 7.6 %copy-start.7 = (bf16[4,1024]{1,0:T(4,128)(2,1)S(1)}, bf16[4,1024]{1,0:T(4,128)(2,1)}, u32[]{:S(2)}) copy-start(bf16[4,1024]{1,0:T(4,128)(2,1)} %param.7) | copy-start | bytes 24580
  0.6 48.5 %all-to-all-start = ((bf16[4,32,6144]{2,0,1:T(4,128)(2,1)}), bf16[4,32,6144]{2,0,1:T(4,128)(2,1)S(1)}, u32[]{:S(2)}, u32[]{:S(2)}) async-start(bf16[4,32,6144]{2,0,1:T(4,128)(2,1)} %bitcast.20), calls=%async_computation | async-start | bytes 3145728 | tf_op jit(solution)/shard_map/all_to_all | solution.py:389
  8.3 1.2 collective-permute-start
  9.6 4.4 %collective-permute-start.1 = (bf16[8,1152]{1,0:T(8,128)(2,1)S(1)}, bf16[8,1152]{1,0:T(8,128)(2,1)S(1)}, u32[]{:S(2)}, u32[]{:S(2)}) collective-permute-start(bf16[8,1152]{1,0:T(8,128)(2,1)S(1)} %pad_maximum_fusion.8), channel_id=1, source_target_pairs={{0,2},{1,3},{2,0},{3,1},{4,6},{5,7},{6,4},{7,5},{8,10},{9,11},{10,... | collective-permute-start | bytes 55304 | tf_op jit(solution)/shard_map/ppermute | solution.py:35
  14.0 25.8 %collective-permute-start.2 = (bf16[16,1152]{1,0:T(8,128)(2,1)S(1)}, bf16[16,1152]{1,0:T(8,128)(2,1)S(1)}, u32[]{:S(2)}, u32[]{:S(2)}) collective-permute-start(bf16[16,1152]{1,0:T(8,128)(2,1)S(1)} %pad_maximum_fusion.7), channel_id=1, source_target_pairs={{0,4},{1,5},{2,6},{3,7},{4,0},{5,1},{6,2},{7,3},{8,12},{9,13},{10,... | collective-permute-start | bytes 110600 | tf_op jit(solution)/shard_map/ppermute | solution.py:35
  39.8 19.3 %copy-start.6 = (bf16[32,1152]{1,0:T(8,128)(2,1)}, bf16[32,1152]{1,0:T(8,128)(2,1)S(1)}, u32[]{:S(2)}) copy-start(bf16[32,1152]{1,0:T(8,128)(2,1)S(1)} %pad_maximum_fusion.6.refs_0_) | copy-start | bytes 221188
  39.9 19.3 %collective-permute-start.5 = (bf16[32,1152]{1,0:T(8,128)(2,1)S(1)}, bf16[32,1152]{1,0:T(8,128)(2,1)S(1)}, u32[]{:S(2)}, u32[]{:S(2)}) collective-permute-start(bf16[32,1152]{1,0:T(8,128)(2,1)S(1)} %pad_maximum_fusion.6.refs_0_), channel_id=1, source_target_pairs={{0,24},{1,25},{2,26},{3,27},{4,28},{5,29},{6,30},{7,31},{8,16},{9,... | collective-permute-start | bytes 221192 | tf_op jit(solution)/shard_map/ppermute | solution.py:35
  41.3 17.8 %collective-permute-start.4 = (bf16[32,1152]{1,0:T(8,128)(2,1)S(1)}, bf16[32,1152]{1,0:T(8,128)(2,1)S(1)}, u32[]{:S(2)}, u32[]{:S(2)}) collective-permute-start(bf16[32,1152]{1,0:T(8,128)(2,1)S(1)} %pad_maximum_fusion.6.refs_0_), channel_id=1, source_target_pairs={{0,16},{1,17},{2,18},{3,19},{4,20},{5,21},{6,22},{7,23},{8,24},{9,... | collective-permute-start | bytes 221192 | tf_op jit(solution)/shard_map/ppermute | solution.py:35
  42.1 17.1 %collective-permute-start.3 = (bf16[32,1152]{1,0:T(8,128)(2,1)S(1)}, bf16[32,1152]{1,0:T(8,128)(2,1)S(1)}, u32[]{:S(2)}, u32[]{:S(2)}) collective-permute-start(bf16[32,1152]{1,0:T(8,128)(2,1)S(1)} %pad_maximum_fusion.6.refs_0_), channel_id=1, source_target_pairs={{0,8},{1,9},{2,10},{3,11},{4,12},{5,13},{6,14},{7,15},{8,0},{9,1},... | collective-permute-start | bytes 221192 | tf_op jit(solution)/shard_map/ppermute | solution.py:35
  59.2 0.6 copy-start.8
  59.2 0.6 copy-start.9
  59.2 0.6 copy-start.10
  64.7 2.3 %collective-permute-start.6 = (bf16[1280,256]{1,0:T(8,128)(2,1)}, bf16[1280,256]{1,0:T(8,128)(2,1)S(1)}, u32[]{:S(2)}, u32[]{:S(2)}) collective-permute-start(bf16[1280,256]{1,0:T(8,128)(2,1)} %get-tuple-element.24), channel_id=1, source_target_pairs={{0,1},{1,0},{2,3},{3,2},{4,5},{5,4},{6,7},{7,6},{8,9},{9,8},{10,11... | collective-permute-start | bytes 1966088 | tf_op jit(solution)/shard_map/ppermute | solution.py:35
  68.5 1.1 copy-start.3
  68.5 9.8 %collective-permute-start.7 = (bf16[640,256]{1,0:T(8,128)(2,1)S(1)}, bf16[640,256]{1,0:T(8,128)(2,1)S(1)}, u32[]{:S(2)}, u32[]{:S(2)}) collective-permute-start(bf16[640,256]{1,0:T(8,128)(2,1)S(1)} %dynamic-slice_convert_fusion.refs_0_), channel_id=1, source_target_pairs={{0,2},{1,3},{2,0},{3,1},{4,6},{5,7},{6,4},{7,5},{8,10},{9,11},{10,... | collective-permute-start | bytes 983048 | tf_op jit(solution)/shard_map/ppermute | solution.py:35
  79.1 1.5 copy-start.5
  79.1 6.2 %collective-permute-start.8 = (bf16[320,256]{1,0:T(8,128)(2,1)S(1)}, bf16[320,256]{1,0:T(8,128)(2,1)S(1)}, u32[]{:S(2)}, u32[]{:S(2)}) collective-permute-start(bf16[320,256]{1,0:T(8,128)(2,1)S(1)} %dynamic-slice_convert_fusion.1.refs_0_), channel_id=1, source_target_pairs={{0,4},{1,5},{2,6},{3,7},{4,0},{5,1},{6,2},{7,3},{8,12},{9,13},{10,... | collective-permute-start | bytes 491528 | tf_op jit(solution)/shard_map/ppermute | solution.py:35
  80.6 10.0 %copy-start.11 = (bf16[16,256]{1,0:T(8,128)(2,1)S(1)}, bf16[16,256]{1,0:T(8,128)(2,1)}, u32[]{:S(2)}) copy-start(bf16[16,256]{1,0:T(8,128)(2,1)} %get-tuple-element.28) | copy-start | bytes 24580
  86.1 4.5 %collective-permute-start.9 = (bf16[160,256]{1,0:T(8,128)(2,1)S(1)}, bf16[160,256]{1,0:T(8,128)(2,1)S(1)}, u32[]{:S(2)}, u32[]{:S(2)}) collective-permute-start(bf16[160,256]{1,0:T(8,128)(2,1)S(1)} %dynamic-slice_convert_fusion.2), channel_id=1, source_target_pairs={{0,8},{1,9},{2,10},{3,11},{4,12},{5,13},{6,14},{7,15},{8,0},{9,1},... | collective-permute-start | bytes 245768 | tf_op jit(solution)/shard_map/ppermute | solution.py:35
  90.6 5.9 %collective-permute-start.10 = (bf16[176,256]{1,0:T(8,128)(2,1)S(1)}, bf16[176,256]{1,0:T(8,128)(2,1)S(1)}, u32[]{:S(2)}, u32[]{:S(2)}) collective-permute-start(bf16[176,256]{1,0:T(8,128)(2,1)S(1)} %pad_maximum_fusion.4), channel_id=1, source_target_pairs={{0,16},{1,17},{2,18},{3,19},{4,20},{5,21},{6,22},{7,23},{8,24},{9,... | collective-permute-start | bytes 270344 | tf_op jit(solution)/shard_map/ppermute | solution.py:35
  96.7 4.6 %collective-permute-start.11 = (bf16[176,256]{1,0:T(8,128)(2,1)S(1)}, bf16[176,256]{1,0:T(8,128)(2,1)S(1)}, u32[]{:S(2)}, u32[]{:S(2)}) collective-permute-start(bf16[176,256]{1,0:T(8,128)(2,1)S(1)} %pad_maximum_fusion.5), channel_id=1, source_target_pairs={{0,8},{1,9},{2,10},{3,11},{4,12},{5,13},{6,14},{7,15},{8,0},{9,1},... | collective-permute-start | bytes 270344 | tf_op jit(solution)/shard_map/ppermute | solution.py:35
  101.3 0.8 copy-start.4
  101.3 6.2 %collective-permute-start.12 = (bf16[352,256]{1,0:T(8,128)(2,1)S(1)}, bf16[352,256]{1,0:T(8,128)(2,1)S(1)}, u32[]{:S(2)}, u32[]{:S(2)}) collective-permute-start(bf16[352,256]{1,0:T(8,128)(2,1)S(1)} %pad_maximum_fusion.3.refs_0_), channel_id=1, source_target_pairs={{0,4},{1,5},{2,6},{3,7},{4,0},{5,1},{6,2},{7,3},{8,12},{9,13},{10,... | collective-permute-start | bytes 540680 | tf_op jit(solution)/shard_map/ppermute | solution.py:35
  107.7 1.8 %copy-start.2 = (bf16[704,256]{1,0:T(8,128)(2,1)}, bf16[704,256]{1,0:T(8,128)(2,1)S(1)}, u32[]{:S(2)}) copy-start(bf16[704,256]{1,0:T(8,128)(2,1)S(1)} %pad_maximum_fusion.2.refs_0_) | copy-start | bytes 1081348
  107.7 9.0 %collective-permute-start.13 = (bf16[704,256]{1,0:T(8,128)(2,1)S(1)}, bf16[704,256]{1,0:T(8,128)(2,1)S(1)}, u32[]{:S(2)}, u32[]{:S(2)}) collective-permute-start(bf16[704,256]{1,0:T(8,128)(2,1)S(1)} %pad_maximum_fusion.2.refs_0_), channel_id=1, source_target_pairs={{0,2},{1,3},{2,0},{3,1},{4,6},{5,7},{6,4},{7,5},{8,10},{9,11},{10,... | collective-permute-start | bytes 1081352 | tf_op jit(solution)/shard_map/ppermute | solution.py:35
  116.0 1.0 copy-start.12
  116.0 1.2 copy-start.13
  116.9 2.3 %collective-permute-start.14 = (bf16[1408,256]{1,0:T(8,128)(2,1)S(1)}, bf16[1408,256]{1,0:T(8,128)(2,1)S(1)}, u32[]{:S(2)}, u32[]{:S(2)}) collective-permute-start(bf16[1408,256]{1,0:T(8,128)(2,1)S(1)} %pad_maximum_fusion.1), channel_id=1, source_target_pairs={{0,1},{1,0},{2,3},{3,2},{4,5},{5,4},{6,7},{7,6},{8,9},{9,8},{10,11... | collective-permute-start | bytes 2162696 | tf_op jit(solution)/shard_map/ppermute | solution.py:35
  119.2 1.0 copy-start.1
  120.1 11.0 %copy-start = (bf16[128,6144]{1,0:T(8,128)(2,1)S(1)}, bf16[128,6144]{1,0:T(8,128)(2,1)}, u32[]{:S(2)}) copy-start(bf16[128,6144]{1,0:T(8,128)(2,1)} %all_to_all.17.columns_ref) | copy-start | bytes 4718596
